TPU v7x, 256 devices: a whole 4x4x8 slice. The times are simulated.
256 devices in a mesh: sink: 32 (over y_lo, z, core), src: 8 (over y_hi, x).
Axes of the slice: x: 4, y: 4 (y_hi: 2, y_lo: 2; y = y_hi * 2 + y_lo), z: 8, core: 2. Of those that a mesh axis runs over, the one named last changes fastest.
Arguments:
- leaf_pos: float32 [2048, 3, 128], P(('sink', 'src')), may hold values from 0 to 4
- leaf_mass: float32 [2048, 128], P(('sink', 'src')), may hold values from 0.3 to 3
- pair_ids: int32 [32, 8, 2, 256], P('sink', 'src'), may hold values from 0 to 2047, as said below
- pair_count: int32 [32, 8], P('sink', 'src'), may hold values from 1 to 256
Outputs:
- force: float32 [2048, 3, 128], P(('sink', 'src'))
Inputs may be any that keep to these rules, and one draw needn't show every extreme that they name: `pair_ids`: in list (s, r) every sink leaf id lies in [s * 8 * 8, (s + 1) * 8 * 8), every source leaf id equals (t * 8 + r) * 8 + k for some t and k < 8, and a slot's two ids differ; dead slots also hold such ids.
All inputs are finite; a program needn't handle non-finite values.
Results may differ from a plain program's by a relative error of at most 0.0001.
Values sent between devices are 32-bit elements; how exact they have to be, the bound alone decides.
A program may use at most 64 MiB of HBM per device.

v0:
```python
import jax
import jax.numpy as jnp
from jax import lax
from jax.sharding import PartitionSpec as P

SOFTEN = 0.09
SPLIT_SCALE = 1.25
GRAVITY = 0.05
TWO_ROOT_PI = 1.1283791670955126
pair_batch = 8


def pair_forces(sink_pos, sink_mass, source_pos, source_mass, live_mask):
    offset = source_pos[:, :, None, :] - sink_pos[:, :, :, None]
    dist_sq = jnp.sum(offset * offset, axis=1) + SOFTEN
    distance = jnp.sqrt(dist_sq)
    scaled = distance * (0.5 / SPLIT_SCALE)
    shaping = jax.scipy.special.erfc(scaled) + TWO_ROOT_PI * scaled * jnp.exp(-scaled * scaled)
    weight_ij = GRAVITY * shaping / (dist_sq * distance)
    weight_ij = (
        weight_ij * sink_mass[:, :, None] * source_mass[:, None, :] * live_mask[:, None, None]
    )
    pulled = weight_ij[:, None, :, :] * offset
    return (jnp.sum(pulled, axis=3), -jnp.sum(pulled, axis=2))


def per_device(leaf_pos, leaf_mass, pair_ids, pair_count):
    local_leaves = leaf_pos.shape[0]
    cells = leaf_pos.shape[2]
    group = lax.axis_size("src")
    row_span = group * local_leaves
    row_pos, row_mass = (
        lax.all_gather(leaf_pos, "src", axis=0, tiled=True),
        lax.all_gather(leaf_mass, "src", axis=0, tiled=True),
    )
    column_pos, column_mass = (
        lax.all_gather(leaf_pos, "sink", axis=0, tiled=True),
        lax.all_gather(leaf_mass, "sink", axis=0, tiled=True),
    )
    sink_ids = pair_ids[0, 0, 0]
    source_ids = pair_ids[0, 0, 1]
    sink_local = sink_ids % row_span
    source_local = source_ids // row_span * local_leaves + source_ids % local_leaves
    count = pair_count[0, 0]
    row_force = jnp.zeros((row_span, 3, cells), jnp.float32)
    column_force = jnp.zeros((column_pos.shape[0], 3, cells), jnp.float32)

    def visit(turn, buffers):
        row_acc, column_acc = buffers
        first = turn * pair_batch
        sinks_here = lax.dynamic_slice_in_dim(sink_local, first, pair_batch)
        sources_here = lax.dynamic_slice_in_dim(source_local, first, pair_batch)
        live_here = (first + jnp.arange(pair_batch, dtype=jnp.int32) < count).astype(jnp.float32)
        force_sink, force_source = pair_forces(
            jnp.take(row_pos, sinks_here, axis=0),
            jnp.take(row_mass, sinks_here, axis=0),
            jnp.take(column_pos, sources_here, axis=0),
            jnp.take(column_mass, sources_here, axis=0),
            live_here,
        )
        return (
            row_acc.at[sinks_here].add(force_sink),
            column_acc.at[sources_here].add(force_source),
        )

    turns = (count + pair_batch - 1) // pair_batch
    row_force, column_force = lax.fori_loop(0, turns, visit, (row_force, column_force))
    mine = lax.psum_scatter(row_force, "src", scatter_dimension=0, tiled=True)
    return mine + lax.psum_scatter(column_force, "sink", scatter_dimension=0, tiled=True)


def solution(mesh):
    return jax.shard_map(
        per_device,
        mesh=mesh,
        in_specs=(
            P(("sink", "src"), None, None),
            P(("sink", "src"), None),
            P("sink", "src", None, None),
            P("sink", "src"),
        ),
        out_specs=P(("sink", "src"), None, None),
        check_vma=False,
    )
```

profile of v0, /device:TPU:1, one launch (start us, length us, event | category | flops | bytes accessed | tf_op | source)
XLA Modules:
  0.0 591.9 jit_solution(6775882339258677780)
XLA Ops:
  7.2 29.3 %all_gather.14 = f32[64,128]{1,0:T(8,128)S(1)} all-gather(f32[8,128]{1,0:T(8,128)} %param.7), channel_id=1, replica_groups=mesh['sink'=32,'src'=8] {'src'}, dimensions={0}, use_global_device_ids=true | all-gather | bytes 36864 | tf_op jit(solution)/shard_map/all_gather | solution.py:34
  36.5 44.1 %all_gather.15 = f32[256,128]{1,0:T(8,128)S(1)} all-gather(f32[8,128]{1,0:T(8,128)} %param.7), channel_id=1, replica_groups=mesh['sink'=32,'src'=8] {'sink'}, dimensions={0}, use_global_device_ids=true | all-gather | bytes 135168 | tf_op jit(solution)/shard_map/all_gather | solution.py:38
  80.6 28.0 %all_gather.13 = f32[64,3,128]{2,0,1:T(8,128)S(1)} all-gather(f32[8,3,128]{2,0,1:T(8,128)} %param.6), channel_id=1, replica_groups=mesh['sink'=32,'src'=8] {'src'}, dimensions={0}, use_global_device_ids=true | all-gather | bytes 110592 | tf_op jit(solution)/shard_map/all_gather | solution.py:33
  108.6 38.1 %all_gather.12 = f32[256,3,128]{2,0,1:T(8,128)S(1)} all-gather(f32[8,3,128]{2,0,1:T(8,128)} %param.6), channel_id=1, replica_groups=mesh['sink'=32,'src'=8] {'sink'}, dimensions={0}, use_global_device_ids=true | all-gather | bytes 405504 | tf_op jit(solution)/shard_map/all_gather | solution.py:37
  147.2 55.7 %while.14 = (s32[]{:T(128)}, f32[64,3,128]{2,1,0:T(4,128)S(1)}, f32[256,3,128]{2,1,0:T(4,128)S(1)}, s32[]{:T(128)}, s32[256]{0:T(256)S(1)}, /*index=5*/s32[256]{...) while((s32[]{:T(128)}, f32[64,3,128]{2,1,0:T(4,128)S(1)}, ...), condition=%wide.region_6.7_spmd, body=%wide.region_0.6_spmd.sunk | while | flops 12203134 | bytes 2417339 | solution.py:67
  151.1 1.5 fusion.28
  152.6 1.0 fusion.29
  159.1 1.5 fusion.28
  160.5 1.0 fusion.29
  161.5 0.8 scatter_fusion
  167.0 1.5 fusion.28
  168.5 1.0 fusion.29
  170.3 0.8 scatter_fusion.1
  175.0 1.5 fusion.28
  176.4 1.0 fusion.29
  182.9 1.5 fusion.28
  184.4 1.0 fusion.29
  190.9 1.5 fusion.28
  192.3 1.0 fusion.29
  198.8 1.5 fusion.28
  200.3 1.0 fusion.29
  204.4 263.8 %reduce-scatter.3.cloned.1.call-done = f32[8,3,128]{2,0,1:T(8,128)} async-done(((f32[64,3,128]{2,0,1:T(8,128)}), f32[8,3,128]{2,0,1:T(8,128)}) %reduce-scatter.3.cloned.1.call-update) | async-done | bytes 12304 | tf_op jit(solution)/shard_map/reduce_scatter | solution.py:68
  468.2 115.5 %reduce-scatter.5.cloned.1.call-done = f32[8,3,128]{2,0,1:T(8,128)} async-done(((f32[256,3,128]{2,0,1:T(8,128)}), f32[8,3,128]{2,0,1:T(8,128)}) %reduce-scatter.5.cloned.1.call-update) | async-done | bytes 12304 | tf_op jit(solution)/shard_map/reduce_scatter | solution.py:69
  583.7 1.3 add.99
  (124 shorter events, 38.3 us)
Async XLA Ops:
  6.5 140.2 %copy-start = (s32[1,1,2,256]{3,2,1,0:T(2,128)S(1)}, s32[1,1,2,256]{3,2,1,0:T(2,128)}, u32[]{:S(2)}) copy-start(s32[1,1,2,256]{3,2,1,0:T(2,128)} %param.8) | copy-start | bytes 6148
  6.5 461.6 %reduce-scatter.3.cloned.1.call-start = ((), (), s32[]{:S(2)}) async-start(), calls=%async_computation.2 | async-start | bytes 110592 | tf_op jit(solution)/shard_map/reduce_scatter | solution.py:68
  203.5 380.1 %reduce-scatter.5.cloned.1.call-start = ((), (), s32[]{:S(2)}) async-start(), calls=%async_computation.3 | async-start | bytes 405504 | tf_op jit(solution)/shard_map/reduce_scatter | solution.py:69
Sparse Core Ops, SparseCore 0:
  203.7 264.4 reduce-scatter.2
  470.7 112.9 reduce-scatter.4
where the time goes:
time: 595 us; the launch traced here: 592 us
  waiting for transfers between devices  379 us (64%)
  blocking collectives  139 us (23%)
  other arithmetic  40.7 us (7%)
  local copies, waits for them, and re-layouts  17.7 us (3%)
  between operations  14.1 us (2%)
    reduce_scatter x1, waiting for transfers between devices, per_device(): mine = lax.psum_scatter(row_force, 'src', scatter_dimension=0, tiled=True)  264 us
    reduce_scatter x1, waiting for transfers between devices, per_device(): lax.psum_scatter(column_force, 'sink', scatter_dimension=0, tiled=True)  116 us
    all_gather x1, blocking collectives, per_device(): lax.all_gather(leaf_mass, 'sink', axis=0, tiled=True)  44.1 us
    all_gather x1, blocking collectives, per_device(): lax.all_gather(leaf_pos, 'sink', axis=0, tiled=True)  38.1 us
    all_gather x1, blocking collectives, per_device(): lax.all_gather(leaf_mass, 'src', axis=0, tiled=True)  29.3 us
    all_gather x1, blocking collectives, per_device(): lax.all_gather(leaf_pos, 'src', axis=0, tiled=True)  28 us
  transfers between devices with their start and end apart: 2, of which 2 were waited for; matrix products, arithmetic and copies ran while one was open for 0% of the time, Pallas kernels for 0%

commit v1 on v0

v1 whole, which is shorter than its diff:
```python
import functools
import math

import jax
import jax.numpy as jnp
from jax import lax
from jax.experimental import pallas as pl
from jax.experimental.pallas import tpu as pltpu
from jax.sharding import PartitionSpec as P

F32 = jnp.float32
BF16 = jnp.bfloat16
SOFTEN = 0.09
LEAF_DEV = 8
CELLS = 128
PAIR_CAP = 256
FIELDS = 32
FORCES = 24
UNROLL = 4
SHAPE = (
    -4.38650632,
    -1.564356609,
    -0.03132662886,
    -0.009803538989,
    -0.002175578276,
    -0.000355445319,
    -4.231931911e-05,
    -3.170157177e-06,
    -1.052514463e-07,
    -2.359194952e-08,
    -4.944213016e-09,
)


def pair_weight(dist_sq):
    scale = jnp.log(dist_sq) * (1.0 / math.log(2.0))
    total = scale * SHAPE[-1] + SHAPE[-2]
    for coef in SHAPE[-3::-1]:
        total = total * scale + coef
    return jnp.exp2(total)


def place():
    return lax.axis_index("sink"), lax.axis_index("src")


def greet(peers):
    barrier = pltpu.get_barrier_semaphore()
    for peer in peers:
        pl.semaphore_signal(
            barrier, inc=1, device_id=peer, device_id_type=pl.DeviceIdType.MESH
        )
    pl.semaphore_wait(barrier, len(peers))


def neighbours(chips, group):
    sink, src = place()
    core = lax.rem(sink, 2)
    chip = sink // 2
    partner = (sink + 1 - 2 * core, src)
    column = [(lax.rem(chip + o, chips) * 2 + core, src) for o in range(1, chips)]
    row = [(sink, lax.rem(src + o, group)) for o in range(1, group)]
    return sink, src, core, chip, partner, column, row


def remote(source, target, send, recv, device):
    return pltpu.make_async_remote_copy(
        src_ref=source,
        dst_ref=target,
        send_sem=send,
        recv_sem=recv,
        device_id=device,
        device_id_type=pl.DeviceIdType.MESH,
    )


def gather_kernel(
    chips, group, pos, mass, ids, count, column_out, rows_out, ids_out,
    pack, column_send, column_recv, row_send, row_recv,
    pass_send, pass_recv, hand_send, hand_recv, own_send, own_recv,
):
    sink, src, core, chip, partner, column, row = neighbours(chips, group)
    greet(column + row + [partner])
    for c in range(3):
        pack[c * 8 : c * 8 + 8, :] = pos[:, c, :]
    pack[24:32, :] = mass[...]
    ids_out[core, 0:2, :] = ids[0, 0, :, 0:128]
    ids_out[core, 2:4, :] = ids[0, 0, :, 128:256]
    ids_out[core, 4:8, :] = jnp.full((4, 128), count[0, 0], jnp.int32)

    sends = []

    def start(copy):
        copy.start()
        sends.append(copy)

    for o, peer in enumerate(column):
        start(remote(pack, column_out.at[sink], column_send.at[o], column_recv.at[o], peer))
    for o, peer in enumerate(row):
        start(remote(pack, rows_out.at[core, src], row_send.at[o], row_recv.at[o], peer))
    start(remote(pack, column_out.at[sink], own_send.at[0], own_recv.at[0], partner))
    start(remote(pack, rows_out.at[core, src], own_send.at[1], own_recv.at[1], partner))
    start(remote(ids_out.at[core], ids_out.at[core], own_send.at[2], own_recv.at[2], partner))
    column_out[sink] = pack[...]
    rows_out[core, src] = pack[...]

    for o in range(1, chips):
        origin = lax.rem(chip + chips - o, chips) * 2 + core
        block = column_out.at[origin]
        remote(pack, block, column_send.at[o - 1], column_recv.at[o - 1], partner).wait_recv()
        start(remote(block, block, pass_send.at[o - 1], pass_recv.at[o - 1], partner))
    for o in range(1, group):
        origin = lax.rem(src + group - o, group)
        block = rows_out.at[core, origin]
        remote(pack, block, row_send.at[o - 1], row_recv.at[o - 1], partner).wait_recv()
        start(remote(block, block, hand_send.at[o - 1], hand_recv.at[o - 1], partner))

    other = 1 - core
    for o in range(1, chips):
        origin = lax.rem(chip + chips - o, chips) * 2 + other
        remote(pack, column_out.at[origin], pass_send.at[o - 1], pass_recv.at[o - 1], partner).wait_recv()
    for o in range(1, group):
        origin = lax.rem(src + group - o, group)
        remote(pack, rows_out.at[other, origin], hand_send.at[o - 1], hand_recv.at[o - 1], partner).wait_recv()
    there = chip * 2 + other
    remote(pack, column_out.at[there], own_send.at[0], own_recv.at[0], partner).wait_recv()
    remote(pack, rows_out.at[other, src], own_send.at[1], own_recv.at[1], partner).wait_recv()
    remote(ids_out.at[other], ids_out.at[other], own_send.at[2], own_recv.at[2], partner).wait_recv()
    for copy in sends:
        copy.wait_send()


def pair_kernel(chips, group, ids, rows, column, row_force, column_force, parts, choose, acc, first_x, second_x):
    blocks = 2 * group
    core = lax.rem(lax.axis_index("sink"), 2)
    column_force[...] = jnp.zeros_like(column_force)
    for h in range(blocks):
        block = rows[h // group, h % group]
        high = block.astype(BF16).astype(F32)
        rest = block - high
        middle = rest.astype(BF16).astype(F32)
        low = rest - middle
        stacked = jnp.concatenate([high, middle, low, jnp.zeros_like(high)], axis=0)
        parts[h] = stacked.T.astype(BF16)
    depth = lax.broadcasted_iota(jnp.int32, (128, 512), 0)
    field = lax.broadcasted_iota(jnp.int32, (128, 512), 1) // 128
    hit = (depth < 96) & (depth % 32 // 8 == field)
    for k in range(8):
        choose[k] = jnp.where(hit & (depth % 8 == k), 1.0, 0.0).astype(BF16)
    for g in range(blocks // 4):
        acc[g] = jnp.zeros((128, 128), F32)
    lane = lax.broadcasted_iota(jnp.int32, (8, 128), 1)

    count_0 = ids[0, 4, 0]
    both = count_0 + ids[1, 4, 0]
    half = (both + 1) // 2
    begin = jnp.where(core == 0, 0, half)
    end = jnp.where(core == 0, half, both)

    def look(slot):
        slot = jnp.minimum(slot, both - 1)
        which = jnp.where(slot < count_0, 0, 1)
        p = slot - which * count_0
        a = ids[which, p // 128 * 2, p % 128]
        b = ids[which, p // 128 * 2 + 1, p % 128]
        sink_block = which * group + a // LEAF_DEV % group
        return sink_block, a % LEAF_DEV, b // (LEAF_DEV * group), b % LEAF_DEV

    def fill(target, first):
        for u in range(UNROLL):
            sink_block, k, _, _ = look(first + u)
            target[u] = jnp.dot(parts[sink_block], choose[k], preferred_element_type=F32)

    def use(spread, first):
        done = []
        for u in range(UNROLL):
            sink_block, k, source_block, source_k = look(first + u)
            live = jnp.where(first + u < end, 1.0, 0.0)
            at = sink_block % 4 * 32 + k
            here = [
                jnp.broadcast_to(column[source_block, pl.ds(8 * c + source_k, 1), :], (8, 128))
                for c in range(4)
            ]
            mass = here[3] * live
            masks = [lane == at + 8 * c for c in range(3)]
            source_sum = [jnp.zeros((8, 128), F32) for _ in range(3)]
            sink_sum = []
            for i in range(0, CELLS, 8):
                there = [spread[u, i : i + 8, 128 * c : 128 * c + 128] for c in range(4)]
                offset = [here[c] - there[c] for c in range(3)]
                dist_sq = (offset[0] * offset[0] + offset[1] * offset[1]) + (
                    offset[2] * offset[2] + SOFTEN
                )
                weight = (pair_weight(dist_sq) * there[3]) * mass
                force = [weight * offset[c] for c in range(3)]
                source_sum = [source_sum[c] + force[c] for c in range(3)]
                total = [jnp.sum(force[c], axis=1, keepdims=True) for c in range(3)]
                sink_sum.append(
                    jnp.where(
                        masks[0],
                        total[0],
                        jnp.where(masks[1], total[1], jnp.where(masks[2], total[2], 0.0)),
                    )
                )
            done.append((sink_block // 4, source_block, source_k, source_sum, sink_sum))
        for g, source_block, source_k, source_sum, sink_sum in done:
            for i, value in enumerate(sink_sum):
                acc[g, pl.ds(8 * i, 8), :] += value
            slot = source_block % 2 * chips + source_block // 2
            for c in range(3):
                column_force[slot, pl.ds(8 * c + source_k, 1), :] -= jnp.sum(
                    source_sum[c], axis=0, keepdims=True
                )

    fill(first_x, begin)

    def turn(i, carry):
        first = begin + i * (2 * UNROLL)
        fill(second_x, first + UNROLL)
        use(first_x, first)
        fill(first_x, first + 2 * UNROLL)
        use(second_x, first + UNROLL)
        return carry

    lax.fori_loop(0, (end - begin + 2 * UNROLL - 1) // (2 * UNROLL), turn, 0)
    for g in range(blocks // 4):
        turned = acc[g].T
        for h in range(4):
            block = g * 4 + h
            row_force[block // group, block % group] = turned[32 * h : 32 * h + FORCES, :]


def reduce_kernel(
    chips, group, row_force, column_force, out,
    row_sum, column_sum, row_in, column_in, swap_row, swap_column,
    column_send, column_recv, row_send, row_recv, swap_send, swap_recv,
):
    sink, src, core, chip, partner, column, row = neighbours(chips, group)
    other = 1 - core
    greet(column + row + [partner])
    to_column = remote(
        column_force.at[pl.ds(other * chips, chips)], swap_column,
        swap_send.at[0], swap_recv.at[0], partner,
    )
    to_row = remote(row_force.at[other], swap_row, swap_send.at[1], swap_recv.at[1], partner)
    to_column.start()
    to_row.start()
    to_column.wait_recv()
    column_sum[...] = column_force[pl.ds(core * chips, chips)] + swap_column[...]
    sends = [to_column, to_row]
    for o, peer in enumerate(column):
        target = lax.rem(chip + o + 1, chips)
        copy = remote(column_sum.at[target], column_in.at[o], column_send.at[o], column_recv.at[o], peer)
        copy.start()
        sends.append(copy)
    to_row.wait_recv()
    row_sum[...] = row_force[core] + swap_row[...]
    for o, peer in enumerate(row):
        target = lax.rem(src + o + 1, group)
        copy = remote(row_sum.at[target], row_in.at[o], row_send.at[o], row_recv.at[o], peer)
        copy.start()
        sends.append(copy)
    total = column_sum[chip] + row_sum[src]
    for o in range(group - 1):
        remote(row_sum.at[0], row_in.at[o], row_send.at[o], row_recv.at[o], partner).wait_recv()
        total = total + row_in[o]
    for o in range(chips - 1):
        remote(column_sum.at[0], column_in.at[o], column_send.at[o], column_recv.at[o], partner).wait_recv()
        total = total + column_in[o]
    for c in range(3):
        out[:, c, :] = total[8 * c : 8 * c + 8, :]
    for copy in sends:
        copy.wait_send()


def per_device(chips, group, leaf_pos, leaf_mass, pair_ids, pair_count):
    vmem = pl.BlockSpec(memory_space=pltpu.VMEM)
    smem = pl.BlockSpec(memory_space=pltpu.SMEM)
    dma = pltpu.SemaphoreType.DMA
    column, rows, ids = pl.pallas_call(
        functools.partial(gather_kernel, chips, group),
        name="gather",
        out_shape=(
            jax.ShapeDtypeStruct((2 * chips, FIELDS, CELLS), F32),
            jax.ShapeDtypeStruct((2, group, FIELDS, CELLS), F32),
            jax.ShapeDtypeStruct((2, 8, CELLS), jnp.int32),
        ),
        in_specs=[vmem, vmem, vmem, smem],
        out_specs=(vmem, vmem, vmem),
        scratch_shapes=[
            pltpu.VMEM((FIELDS, CELLS), F32),
            dma((chips - 1,)), dma((chips - 1,)),
            dma((group - 1,)), dma((group - 1,)),
            dma((chips - 1,)), dma((chips - 1,)),
            dma((group - 1,)), dma((group - 1,)),
            dma((3,)), dma((3,)),
        ],
        compiler_params=pltpu.CompilerParams(
            collective_id=0, has_side_effects=True, vmem_limit_bytes=16 << 20
        ),
    )(leaf_pos, leaf_mass, pair_ids, pair_count)
    blocks = 2 * group
    row_force, column_force = pl.pallas_call(
        functools.partial(pair_kernel, chips, group),
        name="pairs",
        out_shape=(
            jax.ShapeDtypeStruct((2, group, FORCES, CELLS), F32),
            jax.ShapeDtypeStruct((2 * chips, FORCES, CELLS), F32),
        ),
        in_specs=[smem, vmem, vmem],
        out_specs=(vmem, vmem),
        scratch_shapes=[
            pltpu.VMEM((blocks, 128, 128), BF16),
            pltpu.VMEM((8, 128, 512), BF16),
            pltpu.VMEM((blocks // 4, 128, 128), F32),
            pltpu.VMEM((UNROLL, 128, 512), F32),
            pltpu.VMEM((UNROLL, 128, 512), F32),
        ],
        compiler_params=pltpu.CompilerParams(vmem_limit_bytes=40 << 20),
    )(ids, rows, column)
    return pl.pallas_call(
        functools.partial(reduce_kernel, chips, group),
        name="reduce",
        out_shape=jax.ShapeDtypeStruct((LEAF_DEV, 3, CELLS), F32),
        in_specs=[vmem, vmem],
        out_specs=vmem,
        scratch_shapes=[
            pltpu.VMEM((group, FORCES, CELLS), F32),
            pltpu.VMEM((chips, FORCES, CELLS), F32),
            pltpu.VMEM((group - 1, FORCES, CELLS), F32),
            pltpu.VMEM((chips - 1, FORCES, CELLS), F32),
            pltpu.VMEM((group, FORCES, CELLS), F32),
            pltpu.VMEM((chips, FORCES, CELLS), F32),
            dma((chips - 1,)), dma((chips - 1,)),
            dma((group - 1,)), dma((group - 1,)),
            dma((2,)), dma((2,)),
        ],
        compiler_params=pltpu.CompilerParams(
            collective_id=1, has_side_effects=True, vmem_limit_bytes=16 << 20
        ),
    )(row_force, column_force)


def solution(mesh):
    return jax.shard_map(
        functools.partial(per_device, mesh.shape["sink"] // 2, mesh.shape["src"]),
        mesh=mesh,
        in_specs=(
            P(("sink", "src"), None, None),
            P(("sink", "src"), None),
            P("sink", "src", None, None),
            P("sink", "src"),
        ),
        out_specs=P(("sink", "src"), None, None),
        check_vma=False,
    )
```

time: 595 us -> 59.8 us (0.10)
  waiting for transfers between devices: 379 us -> 0 us
  blocking collectives: 139 us -> 0 us
  Pallas kernels: 0 us -> 57.4 us
  other arithmetic: 40.7 us -> 0 us
  local copies, waits for them, and re-layouts: 17.7 us -> 1.33 us
  between operations: 14.1 us -> 0.7 us
    reduce_scatter x2 -> x0, waiting for transfers between devices: 379 us -> none  [the longest x1 264 us: per_device(): mine = lax.psum_scatter(row_force, 'src', scatter_dimension=0, tiled=True)]
    all_gather x4 -> x0, blocking collectives: 139 us -> none  [the longest x1 44.1 us: per_device(): lax.all_gather(leaf_mass, 'sink', axis=0, tiled=True)]
    pallas_call x0 -> x3, Pallas kernels: none -> 57.4 us  [the longest x1 22.3 us: per_device(): pl.pallas_call(functools.partial(gather_kernel, chips, group), name='gath...]
    gather x28 -> x0, local copies, waits for them, and re-layouts: 15.8 us -> none  [the longest x7 4.05 us: visit(): jnp.take(row_pos, sinks_here, axis=0)]
    scatter-add x14 -> x0, other arithmetic: 10.9 us -> none  [the longest x7 5.45 us: visit(): row_acc.at[sinks_here].add(force_sink)]
    reduce_sum x14 -> x0, other arithmetic: 10.4 us -> none  [the longest x7 7.03 us: pair_forces(): return (jnp.sum(pulled, axis=3), -jnp.sum(pulled, axis=2))]
    mul x7 -> x0, other arithmetic: 10.2 us -> none  [pair_forces(): weight_ij * sink_mass[:, :, None] * source_mass[:, None, :]]
  transfers between devices with their start and end apart: 2 -> 0, of which waited for: 2 -> 0; matrix products, arithmetic and copies ran while one was open for 0% -> 0% of each run, Pallas kernels for 0% -> 0%
where the time goes in v1:
time: 59.8 us; the launch traced here: 59.4 us
  Pallas kernels  57.4 us (96%)
  local copies, waits for them, and re-layouts  1.33 us (2%)
  between operations  0.7 us (1%)
    pallas_call x1, Pallas kernels, per_device(): pl.pallas_call(functools.partial(gather_kernel, chips, group), name='gath...  22.3 us
    pallas_call x1, Pallas kernels, per_device(): pl.pallas_call(functools.partial(reduce_kernel, chips, group), name='redu...  19.5 us
    pallas_call x1, Pallas kernels, per_device(): pl.pallas_call(functools.partial(pair_kernel, chips, group), name='pairs'...  15.6 us

profile of v1, /device:TPU:1, one launch (start us, length us, event | category | flops | bytes accessed | tf_op | source)
XLA Modules:
  0.0 59.4 jit_solution(3762864730118304804)
XLA Ops:
  0.7 0.0 copy-start
  0.7 0.0 copy-start.1
  0.7 0.7 %copy.5.pos = f32[8,3,128]{2,1,0:T(4,128)S(1)} copy(f32[8,3,128]{2,0,1:T(8,128)} %param.4) | data formatting | bytes 24576 | tf_op args[0]
  1.4 0.0 copy-done
  1.4 0.0 copy-done.1
  1.4 22.3 %gather.1 = (f32[32,32,128]{2,1,0:T(8,128)S(1)}, f32[2,8,32,128]{3,2,1,0:T(8,128)S(1)}, s32[2,8,128]{2,1,0:T(8,128)S(1)}) custom-call(f32[8,3,128]{2,1,0:T(4,128)S(1)} %copy.5.pos, f32[8,128]{1,0:T(8,128)S(1)} %copy-done, s32[1,1,2,256]{3,2,1,0:T(2,128)S(1)} %copy-done.1, s32[1,1]{1,0:T(1,128)S(6)} %copy.7.count), custom_call_target="tpu_custom_call" | custom-call | tf_op jit(solution)/shard_map/gather/pallas_call | solution.py:280
  23.7 15.6 %pairs.1 = (f32[2,8,24,128]{3,2,1,0:T(8,128)S(1)}, f32[32,24,128]{2,1,0:T(8,128)S(1)}) custom-call(s32[2,8,128]{2,1,0:T(8,128)S(1)} %get-tuple-element.10.ids, f32[2,8,32,128]{3,2,1,0:T(8,128)S(1)} %get-tuple-element.11.rows, f32[32,32,128]{2,1,0:T(8,128)S(1)} %get-tuple-element.12.column), custom_call_target="tpu_custom_call" | custom-call | tf_op jit(solution)/shard_map/pairs/pallas_call | solution.py:303
  39.3 19.5 %reduce.1 = f32[8,3,128]{2,1,0:T(4,128)S(1)} custom-call(f32[2,8,24,128]{3,2,1,0:T(8,128)S(1)} %get-tuple-element.13.row_force, f32[32,24,128]{2,1,0:T(8,128)S(1)} %get-tuple-element.14.column_force), custom_call_target="tpu_custom_call" | custom-call | tf_op jit(solution)/shard_map/reduce/pallas_call | solution.py:321
  58.8 0.6 %copy.6 = f32[8,3,128]{2,0,1:T(8,128)} copy(f32[8,3,128]{2,1,0:T(4,128)S(1)} %reduce.1) | data formatting | bytes 24576 | tf_op jit(solution)/shard_map/reduce/pallas_call | solution.py:321
Async XLA Ops:
  0.7 0.7 %copy-start = (f32[8,128]{1,0:T(8,128)S(1)}, f32[8,128]{1,0:T(8,128)}, u32[]{:S(2)}) copy-start(f32[8,128]{1,0:T(8,128)} %mass.1) | copy-start | bytes 12292
  0.7 0.7 %copy-start.1 = (s32[1,1,2,256]{3,2,1,0:T(2,128)S(1)}, s32[1,1,2,256]{3,2,1,0:T(2,128)}, u32[]{:S(2)}) copy-start(s32[1,1,2,256]{3,2,1,0:T(2,128)} %ids.1) | copy-start | bytes 6148

commit v2 on v1

--- a/solution.py
+++ b/solution.py
@@ -17,27 +17,18 @@
 FIELDS = 32
 FORCES = 24
 UNROLL = 4
-SHAPE = (
-    -4.38650632,
-    -1.564356609,
-    -0.03132662886,
-    -0.009803538989,
-    -0.002175578276,
-    -0.000355445319,
-    -4.231931911e-05,
-    -3.170157177e-06,
-    -1.052514463e-07,
-    -2.359194952e-08,
-    -4.944213016e-09,
-)
+GRAVITY = 0.05
+FALLOFF = 0.16
+TWO_ROOT_PI = 1.1283791670955126
+FACTOR = GRAVITY * FALLOFF**1.5
 
 
 def pair_weight(dist_sq):
-    scale = jnp.log(dist_sq) * (1.0 / math.log(2.0))
-    total = scale * SHAPE[-1] + SHAPE[-2]
-    for coef in SHAPE[-3::-1]:
-        total = total * scale + coef
-    return jnp.exp2(total)
+    square = dist_sq * FALLOFF
+    inverse = lax.rsqrt(square)
+    tail = 1.0 - lax.erf(square * inverse)
+    bell = jnp.exp2(dist_sq * (-FALLOFF / math.log(2.0)))
+    return (tail * inverse + bell * TWO_ROOT_PI) * (inverse * inverse)
 
 
 def place():
@@ -175,7 +166,7 @@
         done = []
         for u in range(UNROLL):
             sink_block, k, source_block, source_k = look(first + u)
-            live = jnp.where(first + u < end, 1.0, 0.0)
+            live = jnp.where(first + u < end, FACTOR, 0.0)
             at = sink_block % 4 * 32 + k
             here = [
                 jnp.broadcast_to(column[source_block, pl.ds(8 * c + source_k, 1), :], (8, 128))

time: 59.8 us -> 57.6 us (0.963)
  the two profiles are of different devices: /device:TPU:1 before, /device:TPU:16 now
where the time goes in v2:
time: 57.6 us; the launch traced here: 57.5 us
  Pallas kernels  55.4 us (96%)
  local copies, waits for them, and re-layouts  1.33 us (2%)
  between operations  0.7 us (1%)
    pallas_call x1, Pallas kernels, per_device(): pl.pallas_call(functools.partial(reduce_kernel, chips, group), name='redu...  24.1 us
    pallas_call x1, Pallas kernels, per_device(): pl.pallas_call(functools.partial(gather_kernel, chips, group), name='gath...  18 us
    pallas_call x1, Pallas kernels, per_device(): pl.pallas_call(functools.partial(pair_kernel, chips, group), name='pairs'...  13.3 us

profile of v2, /device:TPU:16, one launch (start us, length us, event | category | flops | bytes accessed | tf_op | source)
XLA Modules:
  0.0 57.5 jit_solution(8280895792013416995)
XLA Ops:
  0.7 0.0 copy-start
  0.7 0.0 copy-start.1
  0.7 0.7 %copy.5.pos = f32[8,3,128]{2,1,0:T(4,128)S(1)} copy(f32[8,3,128]{2,0,1:T(8,128)} %param.4) | data formatting | bytes 24576 | tf_op args[0]
  1.4 0.0 copy-done
  1.4 0.0 copy-done.1
  1.4 18.0 %gather.1 = (f32[32,32,128]{2,1,0:T(8,128)S(1)}, f32[2,8,32,128]{3,2,1,0:T(8,128)S(1)}, s32[2,8,128]{2,1,0:T(8,128)S(1)}) custom-call(f32[8,3,128]{2,1,0:T(4,128)S(1)} %copy.5.pos, f32[8,128]{1,0:T(8,128)S(1)} %copy-done, s32[1,1,2,256]{3,2,1,0:T(2,128)S(1)} %copy-done.1, s32[1,1]{1,0:T(1,128)S(6)} %copy.7.count), custom_call_target="tpu_custom_call" | custom-call | tf_op jit(solution)/shard_map/gather/pallas_call | solution.py:271
  19.4 13.3 %pairs.1 = (f32[2,8,24,128]{3,2,1,0:T(8,128)S(1)}, f32[32,24,128]{2,1,0:T(8,128)S(1)}) custom-call(s32[2,8,128]{2,1,0:T(8,128)S(1)} %get-tuple-element.10.ids, f32[2,8,32,128]{3,2,1,0:T(8,128)S(1)} %get-tuple-element.11.rows, f32[32,32,128]{2,1,0:T(8,128)S(1)} %get-tuple-element.12.column), custom_call_target="tpu_custom_call" | custom-call | tf_op jit(solution)/shard_map/pairs/pallas_call | solution.py:294
  32.8 24.1 %reduce.1 = f32[8,3,128]{2,1,0:T(4,128)S(1)} custom-call(f32[2,8,24,128]{3,2,1,0:T(8,128)S(1)} %get-tuple-element.13.row_force, f32[32,24,128]{2,1,0:T(8,128)S(1)} %get-tuple-element.14.column_force), custom_call_target="tpu_custom_call" | custom-call | tf_op jit(solution)/shard_map/reduce/pallas_call | solution.py:312
  56.9 0.6 %copy.6 = f32[8,3,128]{2,0,1:T(8,128)} copy(f32[8,3,128]{2,1,0:T(4,128)S(1)} %reduce.1) | data formatting | bytes 24576 | tf_op jit(solution)/shard_map/reduce/pallas_call | solution.py:312
Async XLA Ops:
  0.7 0.7 %copy-start = (f32[8,128]{1,0:T(8,128)S(1)}, f32[8,128]{1,0:T(8,128)}, u32[]{:S(2)}) copy-start(f32[8,128]{1,0:T(8,128)} %mass.1) | copy-start | bytes 12292
  0.7 0.7 %copy-start.1 = (s32[1,1,2,256]{3,2,1,0:T(2,128)S(1)}, s32[1,1,2,256]{3,2,1,0:T(2,128)}, u32[]{:S(2)}) copy-start(s32[1,1,2,256]{3,2,1,0:T(2,128)} %ids.1) | copy-start | bytes 6148

commit v3 on v2

v3 whole, which is shorter than its diff:
```python
import functools
import math

import jax
import jax.numpy as jnp
from jax import lax
from jax.experimental import pallas as pl
from jax.experimental.pallas import tpu as pltpu
from jax.sharding import PartitionSpec as P

F32 = jnp.float32
BF16 = jnp.bfloat16
SOFTEN = 0.09
LEAF_DEV = 8
CELLS = 128
PAIR_CAP = 256
FIELDS = 32
FORCES = 24
UNROLL = 4
GRAVITY = 0.05
FALLOFF = 0.16
TWO_ROOT_PI = 1.1283791670955126
FACTOR = GRAVITY * FALLOFF**1.5


def pair_weight(dist_sq):
    square = dist_sq * FALLOFF
    inverse = lax.rsqrt(square)
    tail = 1.0 - lax.erf(square * inverse)
    bell = jnp.exp2(dist_sq * (-FALLOFF / math.log(2.0)))
    return (tail * inverse + bell * TWO_ROOT_PI) * (inverse * inverse)


def place():
    return lax.axis_index("sink"), lax.axis_index("src")


def greet(peers):
    barrier = pltpu.get_barrier_semaphore()
    for peer in peers:
        pl.semaphore_signal(
            barrier, inc=1, device_id=peer, device_id_type=pl.DeviceIdType.MESH
        )
    pl.semaphore_wait(barrier, len(peers))


def peers_of(chips, group):
    sink, src = place()
    core = lax.rem(sink, 2)
    half = sink // chips
    rings = sorted(range(chips // 2), key=lambda o: -min(o, chips // 2 - o))
    steps = [(h, o) for o in rings for h in (1, 0) if (h, o) != (0, 0)]
    rows = sorted(range(group), key=lambda o: -min(o, group - o))
    return sink, src, core, half, steps, rows


def moved(sink, chips, step, back=False):
    half, ring = step
    ring = chips // 2 - ring if back else ring
    within = lax.rem(lax.rem(sink, chips) // 2 + ring, chips // 2)
    return lax.rem(sink // chips + half, 2) * chips + within * 2 + lax.rem(sink, 2)


def remote(source, target, send, recv, device):
    return pltpu.make_async_remote_copy(
        src_ref=source,
        dst_ref=target,
        send_sem=send,
        recv_sem=recv,
        device_id=device,
        device_id_type=pl.DeviceIdType.MESH,
    )


def gather_kernel(
    chips, group, pos, mass, ids, count, column_out, rows_out, ids_out,
    pack, column_send, column_recv, row_send, row_recv, pass_send, pass_recv,
    hand_send, hand_recv, own_send, own_recv,
):
    sink, src, core, half, steps, rows = peers_of(chips, group)
    other = 1 - core
    across = lax.rem(sink + chips, 2 * chips)
    partner = (sink + 1 - 2 * core, src)
    diagonal = (across + 1 - 2 * core, src)
    column = [(moved(sink, chips, step), src) for step in steps]
    row = [
        (h, o, (across if h else sink, lax.rem(src + o, group)))
        for o in rows for h in (1, 0) if (h, o) != (0, 0)
    ]
    greet(column + [peer for h, o, peer in row if o] + [partner, diagonal])
    pack[0:24, :] = pos[...].reshape(24, CELLS)
    pack[24:32, :] = mass[...]
    mine = core * 2 + half
    ids_out[mine, 0:2, :] = ids[0, 0, :, 0:128]
    ids_out[mine, 2:4, :] = ids[0, 0, :, 128:256]
    ids_out[mine, 4:8, :] = jnp.full((4, 128), count[0, 0], jnp.int32)

    sends = []

    def start(copy):
        copy.start()
        sends.append(copy)

    for i, peer in enumerate(column):
        start(remote(pack, column_out.at[sink], column_send.at[i], column_recv.at[i], peer))
    for i, (h, o, peer) in enumerate(row):
        start(remote(pack, rows_out.at[mine, src], row_send.at[i], row_recv.at[i], peer))
    start(remote(pack, column_out.at[sink], own_send.at[0], own_recv.at[0], partner))
    start(remote(pack, rows_out.at[mine, src], own_send.at[1], own_recv.at[1], partner))
    pool = [partner, (across, src), diagonal]
    for i, peer in enumerate(pool):
        start(remote(ids_out.at[mine], ids_out.at[mine], own_send.at[2 + i], own_recv.at[2 + i], peer))
    column_out[sink] = pack[...]
    rows_out[mine, src] = pack[...]

    for i, (h, o, peer) in reversed(list(enumerate(row))):
        block = rows_out.at[core * 2 + lax.rem(half + h, 2), lax.rem(src + group - o, group)]
        remote(pack, block, row_send.at[i], row_recv.at[i], partner).wait_recv()
        start(remote(block, block, hand_send.at[i], hand_recv.at[i], partner))
    for i, step in reversed(list(enumerate(steps))):
        block = column_out.at[moved(sink, chips, step, back=True)]
        remote(pack, block, column_send.at[i], column_recv.at[i], partner).wait_recv()
        start(remote(block, block, pass_send.at[i], pass_recv.at[i], partner))

    for i, (h, o, peer) in reversed(list(enumerate(row))):
        block = rows_out.at[other * 2 + lax.rem(half + h, 2), lax.rem(src + group - o, group)]
        remote(pack, block, hand_send.at[i], hand_recv.at[i], partner).wait_recv()
    for i, step in reversed(list(enumerate(steps))):
        block = column_out.at[moved(partner[0], chips, step, back=True)]
        remote(pack, block, pass_send.at[i], pass_recv.at[i], partner).wait_recv()
    remote(pack, column_out.at[partner[0]], own_send.at[0], own_recv.at[0], partner).wait_recv()
    remote(pack, rows_out.at[other * 2 + half, src], own_send.at[1], own_recv.at[1], partner).wait_recv()
    origins = [other * 2 + half, core * 2 + 1 - half, other * 2 + 1 - half]
    for i, origin in enumerate(origins):
        remote(ids_out.at[mine], ids_out.at[origin], own_send.at[2 + i], own_recv.at[2 + i], partner).wait_recv()
    for copy in sends:
        copy.wait_send()


def pair_kernel(chips, group, ids, rows, column, row_force, column_force, parts, choose, acc, first_x, second_x):
    sink = lax.axis_index("sink")
    mine = lax.rem(sink, 2) * 2 + sink // chips
    counts = [ids[w, 4, 0] for w in range(4)]
    starts = [0]
    for w in range(4):
        starts.append(starts[w] + counts[w])
    every = starts[4]
    begin = mine * every // 4
    end = (mine + 1) * every // 4
    last = jnp.maximum(end - 1, 0)
    column_force[...] = jnp.zeros_like(column_force)

    for w in range(4):

        @pl.when((starts[w] < end) & (starts[w + 1] > begin))
        def _(w=w):
            for h in range(group):
                block = rows[w, h]
                high = block.astype(BF16).astype(F32)
                rest = block - high
                middle = rest.astype(BF16).astype(F32)
                low = rest - middle
                stacked = jnp.concatenate([high, middle, low, jnp.zeros_like(high)], axis=0)
                parts[w * group + h] = stacked.T.astype(BF16)

    depth = lax.broadcasted_iota(jnp.int32, (128, 512), 0)
    field = lax.broadcasted_iota(jnp.int32, (128, 512), 1) // 128
    hit = (depth < 96) & (depth % 32 // 8 == field)
    for k in range(8):
        choose[k] = jnp.where(hit & (depth % 8 == k), 1.0, 0.0).astype(BF16)
    acc[...] = jnp.zeros_like(acc)
    lane = lax.broadcasted_iota(jnp.int32, (8, 128), 1)

    def look(slot):
        slot = jnp.minimum(slot, last)
        which = sum(jnp.where(slot >= starts[w], 1, 0) for w in range(1, 4))
        p = slot
        for w in range(3):
            p = p - jnp.where(slot >= starts[w + 1], counts[w], 0)
        a = ids[which, p // 128 * 2, p % 128]
        b = ids[which, p // 128 * 2 + 1, p % 128]
        sink_block = which * group + a // LEAF_DEV % group
        return sink_block, a % LEAF_DEV, b // (LEAF_DEV * group), b % LEAF_DEV

    def fill(target, first):
        for u in range(UNROLL):
            sink_block, k, _, _ = look(first + u)
            target[u] = jnp.dot(parts[sink_block], choose[k], preferred_element_type=F32)

    def use(spread, first):
        done = []
        for u in range(UNROLL):
            sink_block, k, source_block, source_k = look(first + u)
            live = jnp.where(first + u < end, FACTOR, 0.0)
            at = sink_block % 4 * 32 + k
            here = [
                jnp.broadcast_to(column[source_block, pl.ds(8 * c + source_k, 1), :], (8, 128))
                for c in range(4)
            ]
            mass = here[3] * live
            masks = [lane == at + 8 * c for c in range(3)]
            source_sum = [jnp.zeros((8, 128), F32) for _ in range(3)]
            sink_sum = []
            for i in range(0, CELLS, 8):
                there = [spread[u, i : i + 8, 128 * c : 128 * c + 128] for c in range(4)]
                offset = [here[c] - there[c] for c in range(3)]
                dist_sq = (offset[0] * offset[0] + offset[1] * offset[1]) + (
                    offset[2] * offset[2] + SOFTEN
                )
                weight = (pair_weight(dist_sq) * there[3]) * mass
                force = [weight * offset[c] for c in range(3)]
                source_sum = [source_sum[c] + force[c] for c in range(3)]
                total = [jnp.sum(force[c], axis=1, keepdims=True) for c in range(3)]
                sink_sum.append(
                    jnp.where(
                        masks[0],
                        total[0],
                        jnp.where(masks[1], total[1], jnp.where(masks[2], total[2], 0.0)),
                    )
                )
            done.append((sink_block // 4, source_block, source_k, source_sum, sink_sum))
        for g, source_block, source_k, source_sum, sink_sum in done:
            for i, value in enumerate(sink_sum):
                acc[g, pl.ds(8 * i, 8), :] += value
            slot = source_block % 2 * chips + source_block // 2
            for c in range(3):
                column_force[slot, pl.ds(8 * c + source_k, 1), :] -= jnp.sum(
                    source_sum[c], axis=0, keepdims=True
                )

    fill(first_x, begin)

    def turn(i, carry):
        first = begin + i * (2 * UNROLL)
        fill(second_x, first + UNROLL)
        use(first_x, first)
        fill(first_x, first + 2 * UNROLL)
        use(second_x, first + UNROLL)
        return carry

    lax.fori_loop(0, (end - begin + 2 * UNROLL - 1) // (2 * UNROLL), turn, 0)
    for w in range(4):
        used = (starts[w] < end) & (starts[w + 1] > begin)

        @pl.when(used)
        def _(w=w):
            for g in range(group // 4):
                turned = acc[w * (group // 4) + g].T
                for h in range(4):
                    row_force[w, g * 4 + h] = turned[32 * h : 32 * h + FORCES, :]

        @pl.when(jnp.logical_not(used))
        def _(w=w):
            row_force[w] = jnp.zeros_like(row_force[w])


def reduce_kernel(
    chips, group, row_force, column_force, out,
    row_sum, column_sum, row_in, column_in, swap_row, swap_column,
    column_send, column_recv, row_send, row_recv, swap_send, swap_recv,
):
    sink, src, core, half, steps, rows = peers_of(chips, group)
    other = 1 - core
    across = lax.rem(sink + chips, 2 * chips)
    partner = (sink + 1 - 2 * core, src)
    column = [(moved(sink, chips, step), src) for step in steps]
    row = [
        (h, o, (across if h else sink, lax.rem(src + o, group)))
        for o in rows for h in (1, 0) if (h, o) != (0, 0)
    ]
    greet(column + [peer for h, o, peer in row if o] + [partner])
    to_column = remote(
        column_force.at[pl.ds(other * chips, chips)], swap_column,
        swap_send.at[0], swap_recv.at[0], partner,
    )
    to_row = remote(
        row_force.at[pl.ds(other * 2, 2)], swap_row, swap_send.at[1], swap_recv.at[1], partner
    )
    to_column.start()
    to_row.start()
    to_column.wait_recv()
    column_sum[...] = column_force[pl.ds(core * chips, chips)] + swap_column[...]
    sends = [to_column, to_row]
    for i, peer in enumerate(column):
        copy = remote(
            column_sum.at[peer[0] // 2], column_in.at[i], column_send.at[i], column_recv.at[i], peer
        )
        copy.start()
        sends.append(copy)
    to_row.wait_recv()
    row_sum[...] = row_force[pl.ds(core * 2, 2)] + swap_row[...]
    for i, (h, o, peer) in enumerate(row):
        copy = remote(
            row_sum.at[lax.rem(half + h, 2), peer[1]], row_in.at[i],
            row_send.at[i], row_recv.at[i], peer,
        )
        copy.start()
        sends.append(copy)
    total = column_sum[sink // 2] + row_sum[half, src]
    for i in reversed(range(len(row))):
        remote(row_sum.at[0, 0], row_in.at[i], row_send.at[i], row_recv.at[i], partner).wait_recv()
        total = total + row_in[i]
    for i in reversed(range(len(column))):
        remote(column_sum.at[0], column_in.at[i], column_send.at[i], column_recv.at[i], partner).wait_recv()
        total = total + column_in[i]
    out[...] = total.reshape(3, LEAF_DEV, CELLS)
    for copy in sends:
        copy.wait_send()


def per_device(chips, group, leaf_pos, leaf_mass, pair_ids, pair_count):
    vmem = pl.BlockSpec(memory_space=pltpu.VMEM)
    smem = pl.BlockSpec(memory_space=pltpu.SMEM)
    dma = pltpu.SemaphoreType.DMA
    column, rows, ids = pl.pallas_call(
        functools.partial(gather_kernel, chips, group),
        name="gather",
        out_shape=(
            jax.ShapeDtypeStruct((2 * chips, FIELDS, CELLS), F32),
            jax.ShapeDtypeStruct((4, group, FIELDS, CELLS), F32),
            jax.ShapeDtypeStruct((4, 8, CELLS), jnp.int32),
        ),
        in_specs=[vmem, vmem, vmem, smem],
        out_specs=(vmem, vmem, vmem),
        scratch_shapes=[
            pltpu.VMEM((FIELDS, CELLS), F32),
            dma((chips - 1,)), dma((chips - 1,)),
            dma((2 * group - 1,)), dma((2 * group - 1,)),
            dma((chips - 1,)), dma((chips - 1,)),
            dma((2 * group - 1,)), dma((2 * group - 1,)),
            dma((5,)), dma((5,)),
        ],
        compiler_params=pltpu.CompilerParams(
            collective_id=0, has_side_effects=True, vmem_limit_bytes=16 << 20
        ),
    )(jnp.transpose(leaf_pos, (1, 0, 2)), leaf_mass, pair_ids, pair_count)
    blocks = 4 * group
    row_force, column_force = pl.pallas_call(
        functools.partial(pair_kernel, chips, group),
        name="pairs",
        out_shape=(
            jax.ShapeDtypeStruct((4, group, FORCES, CELLS), F32),
            jax.ShapeDtypeStruct((2 * chips, FORCES, CELLS), F32),
        ),
        in_specs=[smem, vmem, vmem],
        out_specs=(vmem, vmem),
        scratch_shapes=[
            pltpu.VMEM((blocks, 128, 128), BF16),
            pltpu.VMEM((8, 128, 512), BF16),
            pltpu.VMEM((blocks // 4, 128, 128), F32),
            pltpu.VMEM((UNROLL, 128, 512), F32),
            pltpu.VMEM((UNROLL, 128, 512), F32),
        ],
        compiler_params=pltpu.CompilerParams(vmem_limit_bytes=40 << 20),
    )(ids, rows, column)
    force = pl.pallas_call(
        functools.partial(reduce_kernel, chips, group),
        name="reduce",
        out_shape=jax.ShapeDtypeStruct((3, LEAF_DEV, CELLS), F32),
        in_specs=[vmem, vmem],
        out_specs=vmem,
        scratch_shapes=[
            pltpu.VMEM((2, group, FORCES, CELLS), F32),
            pltpu.VMEM((chips, FORCES, CELLS), F32),
            pltpu.VMEM((2 * group - 1, FORCES, CELLS), F32),
            pltpu.VMEM((chips - 1, FORCES, CELLS), F32),
            pltpu.VMEM((2, group, FORCES, CELLS), F32),
            pltpu.VMEM((chips, FORCES, CELLS), F32),
            dma((chips - 1,)), dma((chips - 1,)),
            dma((2 * group - 1,)), dma((2 * group - 1,)),
            dma((2,)), dma((2,)),
        ],
        compiler_params=pltpu.CompilerParams(
            collective_id=1, has_side_effects=True, vmem_limit_bytes=16 << 20
        ),
    )(row_force, column_force)
    return jnp.transpose(force, (1, 0, 2))


def solution(mesh):
    return jax.shard_map(
        functools.partial(per_device, mesh.shape["sink"] // 2, mesh.shape["src"]),
        mesh=mesh,
        in_specs=(
            P(("sink", "src"), None, None),
            P(("sink", "src"), None),
            P("sink", "src", None, None),
            P("sink", "src"),
        ),
        out_specs=P(("sink", "src"), None, None),
        check_vma=False,
    )
```

time: 57.6 us -> 53.6 us (0.931)
  the two profiles are of different devices: /device:TPU:16 before, /device:TPU:18 now
where the time goes in v3:
time: 53.6 us; the launch traced here: 53.4 us
  Pallas kernels  50.7 us (95%)
  local copies, waits for them, and re-layouts  2.01 us (4%)
  between operations  0.7 us (1%)
    pallas_call x1, Pallas kernels, per_device(): pl.pallas_call(functools.partial(reduce_kernel, chips, group), name='redu...  22.8 us
    pallas_call x1, Pallas kernels, per_device(): pl.pallas_call(functools.partial(gather_kernel, chips, group), name='gath...  17.3 us
    pallas_call x1, Pallas kernels, per_device(): pl.pallas_call(functools.partial(pair_kernel, chips, group), name='pairs'...  10.6 us
    unnamed x7, local copies, waits for them, and re-layouts  2.01 us

profile of v3, /device:TPU:18, one launch (start us, length us, event | category | flops | bytes accessed | tf_op | source)
XLA Modules:
  0.0 53.4 jit_solution(15403210252886379163)
XLA Ops:
  0.0 0.0 copy-start.2
  0.7 0.0 copy-done.2
  0.7 0.0 copy-start
  0.7 0.7 %copy-done = f32[8,3,128]{2,0,1:T(8,128)S(1)} copy-done((f32[8,3,128]{2,0,1:T(8,128)S(1)}, f32[8,3,128]{2,0,1:T(8,128)}, u32[]{:S(2)}) %copy-start) | copy-done | bytes 12312
  1.4 0.0 copy-start.1
  1.4 0.7 %copy-done.1 = f32[8,128]{1,0:T(8,128)S(1)} copy-done((f32[8,128]{1,0:T(8,128)S(1)}, f32[8,128]{1,0:T(8,128)}, u32[]{:S(2)}) %copy-start.1) | copy-done | bytes 4120
  2.1 17.3 %gather.1 = (f32[32,32,128]{2,1,0:T(8,128)S(1)}, f32[4,8,32,128]{3,2,1,0:T(8,128)S(1)}, s32[4,8,128]{2,1,0:T(8,128)S(1)}) custom-call(f32[3,8,128]{2,1,0:T(8,128)S(1)} %bitcast.3, f32[8,128]{1,0:T(8,128)S(1)} %copy-done.1, s32[1,1,2,256]{3,2,1,0:T(2,128)S(1)} %copy-done.2, s32[1,1]{1,0:T(1,128)S(6)} %copy.6.count), custom_call_target="tpu_custom_call" | custom-call | tf_op jit(solution)/shard_map/gather/pallas_call | solution.py:315
  19.4 10.6 %pairs.1 = (f32[4,8,24,128]{3,2,1,0:T(8,128)S(1)}, f32[32,24,128]{2,1,0:T(8,128)S(1)}) custom-call(s32[4,8,128]{2,1,0:T(8,128)S(1)} %get-tuple-element.10.ids, f32[4,8,32,128]{3,2,1,0:T(8,128)S(1)} %get-tuple-element.11.rows, f32[32,32,128]{2,1,0:T(8,128)S(1)} %get-tuple-element.12.column), custom_call_target="tpu_custom_call" | custom-call | tf_op jit(solution)/shard_map/pairs/pallas_call | solution.py:338
  30.0 22.8 %reduce.1 = f32[3,8,128]{2,1,0:T(8,128)S(1)} custom-call(f32[4,8,24,128]{3,2,1,0:T(8,128)S(1)} %get-tuple-element.13.row_force, f32[32,24,128]{2,1,0:T(8,128)S(1)} %get-tuple-element.14.column_force), custom_call_target="tpu_custom_call" | custom-call | tf_op jit(solution)/shard_map/reduce/pallas_call | solution.py:356
  52.8 0.6 %copy.7 = f32[8,3,128]{2,0,1:T(8,128)} copy(f32[8,3,128]{2,0,1:T(8,128)S(1)} %bitcast.2) | data formatting | bytes 24576
Async XLA Ops:
  0.0 0.7 %copy-start.2 = (s32[1,1,2,256]{3,2,1,0:T(2,128)S(1)}, s32[1,1,2,256]{3,2,1,0:T(2,128)}, u32[]{:S(2)}) copy-start(s32[1,1,2,256]{3,2,1,0:T(2,128)} %ids.1) | copy-start | bytes 6148
  0.7 0.7 %copy-start = (f32[8,3,128]{2,0,1:T(8,128)S(1)}, f32[8,3,128]{2,0,1:T(8,128)}, u32[]{:S(2)}) copy-start(f32[8,3,128]{2,0,1:T(8,128)} %param.4) | copy-start | bytes 36868
  1.4 0.7 %copy-start.1 = (f32[8,128]{1,0:T(8,128)S(1)}, f32[8,128]{1,0:T(8,128)}, u32[]{:S(2)}) copy-start(f32[8,128]{1,0:T(8,128)} %mass.1) | copy-start | bytes 12292

commit v4 on v3

--- a/solution.py
+++ b/solution.py
@@ -73,8 +73,8 @@
 
 
 def gather_kernel(
-    chips, group, pos, mass, ids, count, column_out, rows_out, ids_out,
-    pack, column_send, column_recv, row_send, row_recv, pass_send, pass_recv,
+    chips, group, pos, mass, ids, count, column_out, ids_out, parts, choose,
+    rows_out, pack, ids_in, load, column_send, column_recv, row_send, row_recv, pass_send, pass_recv,
     hand_send, hand_recv, own_send, own_recv,
 ):
     sink, src, core, half, steps, rows = peers_of(chips, group)
@@ -87,13 +87,21 @@
         (h, o, (across if h else sink, lax.rem(src + o, group)))
         for o in rows for h in (1, 0) if (h, o) != (0, 0)
     ]
+    loads = [
+        pltpu.make_async_copy(source, target, load.at[i])
+        for i, (source, target) in enumerate((
+            (pos, pack.at[0:3]), (mass, pack.at[3]), (ids, ids_in),
+        ))
+    ]
+    for copy in loads:
+        copy.start()
     greet(column + [peer for h, o, peer in row if o] + [partner, diagonal])
-    pack[0:24, :] = pos[...].reshape(24, CELLS)
-    pack[24:32, :] = mass[...]
+    for copy in loads:
+        copy.wait()
     mine = core * 2 + half
-    ids_out[mine, 0:2, :] = ids[0, 0, :, 0:128]
-    ids_out[mine, 2:4, :] = ids[0, 0, :, 128:256]
-    ids_out[mine, 4:8, :] = jnp.full((4, 128), count[0, 0], jnp.int32)
+    ids_out[mine, 0:2, :] = ids_in[0, 0, :, 0:128]
+    ids_out[mine, 2:4, :] = ids_in[0, 0, :, 128:256]
+    ids_out[mine, 4:8, :] = jnp.full((4, CELLS), count[0, 0], jnp.int32)
 
     sends = []
 
@@ -113,6 +121,21 @@
     column_out[sink] = pack[...]
     rows_out[mine, src] = pack[...]
 
+    depth = lax.broadcasted_iota(jnp.int32, (128, 512), 0)
+    field = lax.broadcasted_iota(jnp.int32, (128, 512), 1) // 128
+    hit = (depth < 96) & (depth % 32 // 8 == field)
+    for k in range(8):
+        choose[k] = jnp.where(hit & (depth % 8 == k), 1.0, 0.0).astype(BF16)
+
+    def split(line, at):
+        block = rows_out[line, at].reshape(FIELDS, CELLS)
+        high = block.astype(BF16).astype(F32)
+        rest = block - high
+        middle = rest.astype(BF16).astype(F32)
+        low = rest - middle
+        stacked = jnp.concatenate([high, middle, low, jnp.zeros_like(high)], axis=0)
+        parts[line, at] = stacked.T.astype(BF16)
+
     for i, (h, o, peer) in reversed(list(enumerate(row))):
         block = rows_out.at[core * 2 + lax.rem(half + h, 2), lax.rem(src + group - o, group)]
         remote(pack, block, row_send.at[i], row_recv.at[i], partner).wait_recv()
@@ -121,15 +144,19 @@
         block = column_out.at[moved(sink, chips, step, back=True)]
         remote(pack, block, column_send.at[i], column_recv.at[i], partner).wait_recv()
         start(remote(block, block, pass_send.at[i], pass_recv.at[i], partner))
+        split(core * 2 + i // group, i % group)
+    split(core * 2 + 1, group - 1)
 
     for i, (h, o, peer) in reversed(list(enumerate(row))):
         block = rows_out.at[other * 2 + lax.rem(half + h, 2), lax.rem(src + group - o, group)]
         remote(pack, block, hand_send.at[i], hand_recv.at[i], partner).wait_recv()
+    remote(pack, rows_out.at[other * 2 + half, src], own_send.at[1], own_recv.at[1], partner).wait_recv()
+    for i in range(2 * group):
+        split(other * 2 + i // group, i % group)
     for i, step in reversed(list(enumerate(steps))):
         block = column_out.at[moved(partner[0], chips, step, back=True)]
         remote(pack, block, pass_send.at[i], pass_recv.at[i], partner).wait_recv()
     remote(pack, column_out.at[partner[0]], own_send.at[0], own_recv.at[0], partner).wait_recv()
-    remote(pack, rows_out.at[other * 2 + half, src], own_send.at[1], own_recv.at[1], partner).wait_recv()
     origins = [other * 2 + half, core * 2 + 1 - half, other * 2 + 1 - half]
     for i, origin in enumerate(origins):
         remote(ids_out.at[mine], ids_out.at[origin], own_send.at[2 + i], own_recv.at[2 + i], partner).wait_recv()
@@ -137,7 +164,9 @@
         copy.wait_send()
 
 
-def pair_kernel(chips, group, ids, rows, column, row_force, column_force, parts, choose, acc, first_x, second_x):
+def pair_kernel(
+    chips, group, ids, parts, choose, column, row_force, column_force, acc, first_x, second_x
+):
     sink = lax.axis_index("sink")
     mine = lax.rem(sink, 2) * 2 + sink // chips
     counts = [ids[w, 4, 0] for w in range(4)]
@@ -150,24 +179,6 @@
     last = jnp.maximum(end - 1, 0)
     column_force[...] = jnp.zeros_like(column_force)
 
-    for w in range(4):
-
-        @pl.when((starts[w] < end) & (starts[w + 1] > begin))
-        def _(w=w):
-            for h in range(group):
-                block = rows[w, h]
-                high = block.astype(BF16).astype(F32)
-                rest = block - high
-                middle = rest.astype(BF16).astype(F32)
-                low = rest - middle
-                stacked = jnp.concatenate([high, middle, low, jnp.zeros_like(high)], axis=0)
-                parts[w * group + h] = stacked.T.astype(BF16)
-
-    depth = lax.broadcasted_iota(jnp.int32, (128, 512), 0)
-    field = lax.broadcasted_iota(jnp.int32, (128, 512), 1) // 128
-    hit = (depth < 96) & (depth % 32 // 8 == field)
-    for k in range(8):
-        choose[k] = jnp.where(hit & (depth % 8 == k), 1.0, 0.0).astype(BF16)
     acc[...] = jnp.zeros_like(acc)
     lane = lax.broadcasted_iota(jnp.int32, (8, 128), 1)
 
@@ -185,7 +196,7 @@
     def fill(target, first):
         for u in range(UNROLL):
             sink_block, k, _, _ = look(first + u)
-            target[u] = jnp.dot(parts[sink_block], choose[k], preferred_element_type=F32)
+            target[u] = jnp.dot(parts[sink_block // group, sink_block % group], choose[k], preferred_element_type=F32)
 
     def use(spread, first):
         done = []
@@ -194,7 +205,7 @@
             live = jnp.where(first + u < end, FACTOR, 0.0)
             at = sink_block % 4 * 32 + k
             here = [
-                jnp.broadcast_to(column[source_block, pl.ds(8 * c + source_k, 1), :], (8, 128))
+                jnp.broadcast_to(column[source_block, c, pl.ds(source_k, 1), :], (8, 128))
                 for c in range(4)
             ]
             mass = here[3] * live
@@ -311,19 +322,24 @@
 def per_device(chips, group, leaf_pos, leaf_mass, pair_ids, pair_count):
     vmem = pl.BlockSpec(memory_space=pltpu.VMEM)
     smem = pl.BlockSpec(memory_space=pltpu.SMEM)
+    hbm = pl.BlockSpec(memory_space=pltpu.HBM)
     dma = pltpu.SemaphoreType.DMA
-    column, rows, ids = pl.pallas_call(
+    column, ids, parts, choose = pl.pallas_call(
         functools.partial(gather_kernel, chips, group),
         name="gather",
         out_shape=(
-            jax.ShapeDtypeStruct((2 * chips, FIELDS, CELLS), F32),
-            jax.ShapeDtypeStruct((4, group, FIELDS, CELLS), F32),
+            jax.ShapeDtypeStruct((2 * chips, 4, LEAF_DEV, CELLS), F32),
             jax.ShapeDtypeStruct((4, 8, CELLS), jnp.int32),
+            jax.ShapeDtypeStruct((4, group, 128, 128), BF16),
+            jax.ShapeDtypeStruct((8, 128, 512), BF16),
         ),
-        in_specs=[vmem, vmem, vmem, smem],
-        out_specs=(vmem, vmem, vmem),
+        in_specs=[hbm] * 3 + [smem],
+        out_specs=(vmem,) * 4,
         scratch_shapes=[
-            pltpu.VMEM((FIELDS, CELLS), F32),
+            pltpu.VMEM((4, group, 4, LEAF_DEV, CELLS), F32),
+            pltpu.VMEM((4, LEAF_DEV, CELLS), F32),
+            pltpu.VMEM((1, 1, 2, PAIR_CAP), jnp.int32),
+            dma((3,)),
             dma((chips - 1,)), dma((chips - 1,)),
             dma((2 * group - 1,)), dma((2 * group - 1,)),
             dma((chips - 1,)), dma((chips - 1,)),
@@ -333,7 +349,10 @@
         compiler_params=pltpu.CompilerParams(
             collective_id=0, has_side_effects=True, vmem_limit_bytes=16 << 20
         ),
-    )(jnp.transpose(leaf_pos, (1, 0, 2)), leaf_mass, pair_ids, pair_count)
+    )(*(
+        pltpu.with_memory_space_constraint(x, pltpu.HBM)
+        for x in (jnp.transpose(leaf_pos, (1, 0, 2)), leaf_mass, pair_ids)
+    ), pair_count)
     blocks = 4 * group
     row_force, column_force = pl.pallas_call(
         functools.partial(pair_kernel, chips, group),
@@ -342,17 +361,15 @@
             jax.ShapeDtypeStruct((4, group, FORCES, CELLS), F32),
             jax.ShapeDtypeStruct((2 * chips, FORCES, CELLS), F32),
         ),
-        in_specs=[smem, vmem, vmem],
+        in_specs=[smem, vmem, vmem, vmem],
         out_specs=(vmem, vmem),
         scratch_shapes=[
-            pltpu.VMEM((blocks, 128, 128), BF16),
-            pltpu.VMEM((8, 128, 512), BF16),
             pltpu.VMEM((blocks // 4, 128, 128), F32),
             pltpu.VMEM((UNROLL, 128, 512), F32),
             pltpu.VMEM((UNROLL, 128, 512), F32),
         ],
         compiler_params=pltpu.CompilerParams(vmem_limit_bytes=40 << 20),
-    )(ids, rows, column)
+    )(ids, parts, choose, column)
     force = pl.pallas_call(
         functools.partial(reduce_kernel, chips, group),
         name="reduce",

time: 53.6 us -> 54.1 us (level)
  the two profiles are of different devices: /device:TPU:18 before, /device:TPU:1 now
where the time goes in v4:
time: 54.1 us; the launch traced here: 54 us
  Pallas kernels  52.7 us (97%)
  between operations  0.68 us (1%)
  local copies, waits for them, and re-layouts  0.6 us (1%)
    pallas_call x1, Pallas kernels, per_device(): pl.pallas_call(functools.partial(gather_kernel, chips, group), name='gath...  22.5 us
    pallas_call x1, Pallas kernels, per_device(): pl.pallas_call(functools.partial(reduce_kernel, chips, group), name='redu...  20.7 us
    pallas_call x1, Pallas kernels, per_device(): pl.pallas_call(functools.partial(pair_kernel, chips, group), name='pairs'...  9.53 us

profile of v4, /device:TPU:1, one launch (start us, length us, event | category | flops | bytes accessed | tf_op | source)
XLA Modules:
  0.0 54.0 jit_solution(11908317674492724175)
XLA Ops:
  0.7 22.5 %gather.1 = (f32[32,4,8,128]{3,2,1,0:T(8,128)S(1)}, s32[4,8,128]{2,1,0:T(8,128)S(1)}, bf16[4,8,128,128]{3,2,1,0:T(8,128)(2,1)S(1)}, bf16[8,128,512]{2,1,0:T(8,128)(2,1)S(1)}) custom-call(f32[3,8,128]{2,1,0:T(8,128)} %bitcast.3, f32[8,128]{1,0:T(8,128)} %mass.1, s32[1,1,2,256]{3,2,1,0:T(2,128)} %ids.1, s32[1,1]{1,0:T(1,128)S(6)} %copy.6.count), custom_call_target="tpu_custom_call" | custom-call | tf_op jit(solution)/shard_map/gather/pallas_call | solution.py:327
  23.2 9.5 %pairs.1 = (f32[4,8,24,128]{3,2,1,0:T(8,128)S(1)}, f32[32,24,128]{2,1,0:T(8,128)S(1)}) custom-call(s32[4,8,128]{2,1,0:T(8,128)S(1)} %get-tuple-element.11.ids, bf16[4,8,128,128]{3,2,1,0:T(8,128)(2,1)S(1)} %get-tuple-element.12.parts, bf16[8,128,512]{2,1,0:T(8,128)(2,1)S(1)} %get-tuple-element.13.choose, f32[32,4,8,128]{3,2,1,0:T(8,128)S(1)} %get-tuple-element.14.column), custom_call_target="tpu_custom_call" | custom-call | tf_op jit(solution)/shard_map/pairs/pallas_call | solution.py:357
  32.7 20.7 %reduce.1 = f32[3,8,128]{2,1,0:T(8,128)S(1)} custom-call(f32[4,8,24,128]{3,2,1,0:T(8,128)S(1)} %get-tuple-element.15.row_force, f32[32,24,128]{2,1,0:T(8,128)S(1)} %get-tuple-element.16.column_force), custom_call_target="tpu_custom_call" | custom-call | tf_op jit(solution)/shard_map/reduce/pallas_call | solution.py:373
  53.4 0.6 %copy.7 = f32[8,3,128]{2,0,1:T(8,128)} copy(f32[8,3,128]{2,0,1:T(8,128)S(1)} %bitcast.2) | data formatting | bytes 24576

commit v5 on v3

--- a/solution.py
+++ b/solution.py
@@ -61,6 +61,10 @@
     return lax.rem(sink // chips + half, 2) * chips + within * 2 + lax.rem(sink, 2)
 
 
+def place_of(sink, chips):
+    return lax.rem(sink, 2) * chips + sink // 2
+
+
 def remote(source, target, send, recv, device):
     return pltpu.make_async_remote_copy(
         src_ref=source,
@@ -73,8 +77,8 @@
 
 
 def gather_kernel(
-    chips, group, pos, mass, ids, count, column_out, rows_out, ids_out,
-    pack, column_send, column_recv, row_send, row_recv, pass_send, pass_recv,
+    chips, group, pos, mass, ids, count, column_out, codes, rows_out,
+    ids_out, pack, ids_in, load, column_send, column_recv, row_send, row_recv, pass_send, pass_recv,
     hand_send, hand_recv, own_send, own_recv,
 ):
     sink, src, core, half, steps, rows = peers_of(chips, group)
@@ -87,13 +91,21 @@
         (h, o, (across if h else sink, lax.rem(src + o, group)))
         for o in rows for h in (1, 0) if (h, o) != (0, 0)
     ]
+    loads = [
+        pltpu.make_async_copy(source, target, load.at[i])
+        for i, (source, target) in enumerate((
+            (pos, pack.at[0:3]), (mass, pack.at[3]), (ids, ids_in),
+        ))
+    ]
+    for copy in loads:
+        copy.start()
     greet(column + [peer for h, o, peer in row if o] + [partner, diagonal])
-    pack[0:24, :] = pos[...].reshape(24, CELLS)
-    pack[24:32, :] = mass[...]
+    for copy in loads:
+        copy.wait()
     mine = core * 2 + half
-    ids_out[mine, 0:2, :] = ids[0, 0, :, 0:128]
-    ids_out[mine, 2:4, :] = ids[0, 0, :, 128:256]
-    ids_out[mine, 4:8, :] = jnp.full((4, 128), count[0, 0], jnp.int32)
+    ids_out[mine, 0:2, :] = ids_in[0, 0, :, 0:128]
+    ids_out[mine, 2:4, :] = ids_in[0, 0, :, 128:256]
+    ids_out[mine, 4:8, :] = jnp.full((4, CELLS), count[0, 0], jnp.int32)
 
     sends = []
 
@@ -102,15 +114,15 @@
         sends.append(copy)
 
     for i, peer in enumerate(column):
-        start(remote(pack, column_out.at[sink], column_send.at[i], column_recv.at[i], peer))
+        start(remote(pack, column_out.at[place_of(sink, chips)], column_send.at[i], column_recv.at[i], peer))
     for i, (h, o, peer) in enumerate(row):
         start(remote(pack, rows_out.at[mine, src], row_send.at[i], row_recv.at[i], peer))
-    start(remote(pack, column_out.at[sink], own_send.at[0], own_recv.at[0], partner))
+    start(remote(pack, column_out.at[place_of(sink, chips)], own_send.at[0], own_recv.at[0], partner))
     start(remote(pack, rows_out.at[mine, src], own_send.at[1], own_recv.at[1], partner))
     pool = [partner, (across, src), diagonal]
     for i, peer in enumerate(pool):
         start(remote(ids_out.at[mine], ids_out.at[mine], own_send.at[2 + i], own_recv.at[2 + i], peer))
-    column_out[sink] = pack[...]
+    column_out[place_of(sink, chips)] = pack[...]
     rows_out[mine, src] = pack[...]
 
     for i, (h, o, peer) in reversed(list(enumerate(row))):
@@ -118,83 +130,96 @@
         remote(pack, block, row_send.at[i], row_recv.at[i], partner).wait_recv()
         start(remote(block, block, hand_send.at[i], hand_recv.at[i], partner))
     for i, step in reversed(list(enumerate(steps))):
-        block = column_out.at[moved(sink, chips, step, back=True)]
+        block = column_out.at[place_of(moved(sink, chips, step, back=True), chips)]
         remote(pack, block, column_send.at[i], column_recv.at[i], partner).wait_recv()
         start(remote(block, block, pass_send.at[i], pass_recv.at[i], partner))
 
     for i, (h, o, peer) in reversed(list(enumerate(row))):
         block = rows_out.at[other * 2 + lax.rem(half + h, 2), lax.rem(src + group - o, group)]
         remote(pack, block, hand_send.at[i], hand_recv.at[i], partner).wait_recv()
+    remote(pack, rows_out.at[other * 2 + half, src], own_send.at[1], own_recv.at[1], partner).wait_recv()
     for i, step in reversed(list(enumerate(steps))):
-        block = column_out.at[moved(partner[0], chips, step, back=True)]
+        block = column_out.at[place_of(moved(partner[0], chips, step, back=True), chips)]
         remote(pack, block, pass_send.at[i], pass_recv.at[i], partner).wait_recv()
-    remote(pack, column_out.at[partner[0]], own_send.at[0], own_recv.at[0], partner).wait_recv()
-    remote(pack, rows_out.at[other * 2 + half, src], own_send.at[1], own_recv.at[1], partner).wait_recv()
+    remote(pack, column_out.at[place_of(partner[0], chips)], own_send.at[0], own_recv.at[0], partner).wait_recv()
     origins = [other * 2 + half, core * 2 + 1 - half, other * 2 + 1 - half]
     for i, origin in enumerate(origins):
         remote(ids_out.at[mine], ids_out.at[origin], own_send.at[2 + i], own_recv.at[2 + i], partner).wait_recv()
+    for w in range(4):
+        for h in range(2):
+            a = ids_out[w, 2 * h : 2 * h + 1, :]
+            b = ids_out[w, 2 * h + 1 : 2 * h + 2, :]
+            owner = b // (LEAF_DEV * group)
+            source = (owner % 2 * chips + owner // 2) * LEAF_DEV + b % LEAF_DEV
+            target = w * group * LEAF_DEV + a % (group * LEAF_DEV)
+            codes[2 * w + h : 2 * w + h + 1, :] = target * 256 + source
+        codes[8 + w : 9 + w, :] = ids_out[w, 4:5, :]
     for copy in sends:
         copy.wait_send()
 
 
-def pair_kernel(chips, group, ids, rows, column, row_force, column_force, parts, choose, acc, first_x, second_x):
+def pair_kernel(
+    chips, group, ids, rows_out, column, row_force, column_force, parts, choose, acc, first_x, second_x
+):
     sink = lax.axis_index("sink")
     mine = lax.rem(sink, 2) * 2 + sink // chips
-    counts = [ids[w, 4, 0] for w in range(4)]
     starts = [0]
     for w in range(4):
-        starts.append(starts[w] + counts[w])
+        starts.append(starts[w] + ids[8 + w, 0])
     every = starts[4]
     begin = mine * every // 4
     end = (mine + 1) * every // 4
     last = jnp.maximum(end - 1, 0)
     column_force[...] = jnp.zeros_like(column_force)
-
-    for w in range(4):
-
-        @pl.when((starts[w] < end) & (starts[w + 1] > begin))
-        def _(w=w):
-            for h in range(group):
-                block = rows[w, h]
-                high = block.astype(BF16).astype(F32)
-                rest = block - high
-                middle = rest.astype(BF16).astype(F32)
-                low = rest - middle
-                stacked = jnp.concatenate([high, middle, low, jnp.zeros_like(high)], axis=0)
-                parts[w * group + h] = stacked.T.astype(BF16)
-
     depth = lax.broadcasted_iota(jnp.int32, (128, 512), 0)
     field = lax.broadcasted_iota(jnp.int32, (128, 512), 1) // 128
     hit = (depth < 96) & (depth % 32 // 8 == field)
     for k in range(8):
         choose[k] = jnp.where(hit & (depth % 8 == k), 1.0, 0.0).astype(BF16)
+
+    def split(line, at):
+        block = rows_out[line, at].reshape(FIELDS, CELLS)
+        high = block.astype(BF16).astype(F32)
+        rest = block - high
+        middle = rest.astype(BF16).astype(F32)
+        low = rest - middle
+        stacked = jnp.concatenate([high, middle, low, jnp.zeros_like(high)], axis=0)
+        parts[line * group + at] = stacked.T.astype(BF16)
+
+    for w in range(4):
+
+        @pl.when((starts[w] < end) & (starts[w + 1] > begin))
+        def _(w=w):
+            for h in range(group):
+                split(w, h)
+
+
     acc[...] = jnp.zeros_like(acc)
     lane = lax.broadcasted_iota(jnp.int32, (8, 128), 1)
 
     def look(slot):
         slot = jnp.minimum(slot, last)
-        which = sum(jnp.where(slot >= starts[w], 1, 0) for w in range(1, 4))
-        p = slot
-        for w in range(3):
-            p = p - jnp.where(slot >= starts[w + 1], counts[w], 0)
-        a = ids[which, p // 128 * 2, p % 128]
-        b = ids[which, p // 128 * 2 + 1, p % 128]
-        sink_block = which * group + a // LEAF_DEV % group
-        return sink_block, a % LEAF_DEV, b // (LEAF_DEV * group), b % LEAF_DEV
+        shift = 0
+        for w in range(1, 4):
+            shift = jnp.where(slot >= starts[w], w * PAIR_CAP - starts[w], shift)
+        slot = slot + shift
+        return ids[slot >> 7, slot & 127]
 
     def fill(target, first):
         for u in range(UNROLL):
-            sink_block, k, _, _ = look(first + u)
-            target[u] = jnp.dot(parts[sink_block], choose[k], preferred_element_type=F32)
+            code = look(first + u)
+            target[u] = jnp.dot(parts[code >> 11], choose[code >> 8 & 7], preferred_element_type=F32)
 
     def use(spread, first):
         done = []
         for u in range(UNROLL):
-            sink_block, k, source_block, source_k = look(first + u)
+            code = look(first + u)
+            source_block = code >> 3 & 31
+            source_k = code & 7
             live = jnp.where(first + u < end, FACTOR, 0.0)
-            at = sink_block % 4 * 32 + k
+            at = (code >> 11 & 3) * 32 + (code >> 8 & 7)
             here = [
-                jnp.broadcast_to(column[source_block, pl.ds(8 * c + source_k, 1), :], (8, 128))
+                jnp.broadcast_to(column[source_block, c, pl.ds(source_k, 1), :], (8, 128))
                 for c in range(4)
             ]
             mass = here[3] * live
@@ -218,13 +243,12 @@
                         jnp.where(masks[1], total[1], jnp.where(masks[2], total[2], 0.0)),
                     )
                 )
-            done.append((sink_block // 4, source_block, source_k, source_sum, sink_sum))
+            done.append((code >> 13, source_block, source_k, source_sum, sink_sum))
         for g, source_block, source_k, source_sum, sink_sum in done:
             for i, value in enumerate(sink_sum):
                 acc[g, pl.ds(8 * i, 8), :] += value
-            slot = source_block % 2 * chips + source_block // 2
             for c in range(3):
-                column_force[slot, pl.ds(8 * c + source_k, 1), :] -= jnp.sum(
+                column_force[source_block, pl.ds(8 * c + source_k, 1), :] -= jnp.sum(
                     source_sum[c], axis=0, keepdims=True
                 )
 
@@ -311,19 +335,23 @@
 def per_device(chips, group, leaf_pos, leaf_mass, pair_ids, pair_count):
     vmem = pl.BlockSpec(memory_space=pltpu.VMEM)
     smem = pl.BlockSpec(memory_space=pltpu.SMEM)
+    hbm = pl.BlockSpec(memory_space=pltpu.HBM)
     dma = pltpu.SemaphoreType.DMA
-    column, rows, ids = pl.pallas_call(
+    column, codes, rows = pl.pallas_call(
         functools.partial(gather_kernel, chips, group),
         name="gather",
         out_shape=(
-            jax.ShapeDtypeStruct((2 * chips, FIELDS, CELLS), F32),
-            jax.ShapeDtypeStruct((4, group, FIELDS, CELLS), F32),
-            jax.ShapeDtypeStruct((4, 8, CELLS), jnp.int32),
+            jax.ShapeDtypeStruct((2 * chips, 4, LEAF_DEV, CELLS), F32),
+            jax.ShapeDtypeStruct((16, CELLS), jnp.int32),
+            jax.ShapeDtypeStruct((4, group, 4, LEAF_DEV, CELLS), F32),
         ),
-        in_specs=[vmem, vmem, vmem, smem],
-        out_specs=(vmem, vmem, vmem),
+        in_specs=[hbm] * 3 + [smem],
+        out_specs=(vmem,) * 3,
         scratch_shapes=[
-            pltpu.VMEM((FIELDS, CELLS), F32),
+            pltpu.VMEM((4, 8, CELLS), jnp.int32),
+            pltpu.VMEM((4, LEAF_DEV, CELLS), F32),
+            pltpu.VMEM((1, 1, 2, PAIR_CAP), jnp.int32),
+            dma((3,)),
             dma((chips - 1,)), dma((chips - 1,)),
             dma((2 * group - 1,)), dma((2 * group - 1,)),
             dma((chips - 1,)), dma((chips - 1,)),
@@ -333,7 +361,10 @@
         compiler_params=pltpu.CompilerParams(
             collective_id=0, has_side_effects=True, vmem_limit_bytes=16 << 20
         ),
-    )(jnp.transpose(leaf_pos, (1, 0, 2)), leaf_mass, pair_ids, pair_count)
+    )(*(
+        pltpu.with_memory_space_constraint(x, pltpu.HBM)
+        for x in (jnp.transpose(leaf_pos, (1, 0, 2)), leaf_mass, pair_ids)
+    ), pair_count)
     blocks = 4 * group
     row_force, column_force = pl.pallas_call(
         functools.partial(pair_kernel, chips, group),
@@ -345,14 +376,14 @@
         in_specs=[smem, vmem, vmem],
         out_specs=(vmem, vmem),
         scratch_shapes=[
-            pltpu.VMEM((blocks, 128, 128), BF16),
+            pltpu.VMEM((4 * group, 128, 128), BF16),
             pltpu.VMEM((8, 128, 512), BF16),
             pltpu.VMEM((blocks // 4, 128, 128), F32),
             pltpu.VMEM((UNROLL, 128, 512), F32),
             pltpu.VMEM((UNROLL, 128, 512), F32),
         ],
         compiler_params=pltpu.CompilerParams(vmem_limit_bytes=40 << 20),
-    )(ids, rows, column)
+    )(codes, rows, column)
     force = pl.pallas_call(
         functools.partial(reduce_kernel, chips, group),
         name="reduce",

time: 53.6 us -> 50.7 us (0.946)
  the two profiles are of different devices: /device:TPU:18 before, /device:TPU:2 now
where the time goes in v5:
time: 50.7 us; the launch traced here: 50.6 us
  Pallas kernels  49.3 us (97%)
  between operations  0.68 us (1%)
  local copies, waits for them, and re-layouts  0.6 us (1%)
    pallas_call x1, Pallas kernels, per_device(): pl.pallas_call(functools.partial(gather_kernel, chips, group), name='gath...  19.3 us
    pallas_call x1, Pallas kernels, per_device(): pl.pallas_call(functools.partial(reduce_kernel, chips, group), name='redu...  18.2 us
    pallas_call x1, Pallas kernels, per_device(): pl.pallas_call(functools.partial(pair_kernel, chips, group), name='pairs'...  11.8 us

profile of v5, /device:TPU:2, one launch (start us, length us, event | category | flops | bytes accessed | tf_op | source)
XLA Modules:
  0.0 50.6 jit_solution(7386129967802070885)
XLA Ops:
  0.7 19.3 %gather.1 = (f32[32,4,8,128]{3,2,1,0:T(8,128)S(1)}, s32[16,128]{1,0:T(8,128)S(1)}, f32[4,8,4,8,128]{4,3,2,1,0:T(8,128)S(1)}) custom-call(f32[3,8,128]{2,1,0:T(8,128)} %bitcast.3, f32[8,128]{1,0:T(8,128)} %mass.1, s32[1,1,2,256]{3,2,1,0:T(2,128)} %ids.1, s32[1,1]{1,0:T(1,128)S(6)} %copy.6.count), custom_call_target="tpu_custom_call" | custom-call | tf_op jit(solution)/shard_map/gather/pallas_call | solution.py:340
  20.0 11.8 %pairs.1 = (f32[4,8,24,128]{3,2,1,0:T(8,128)S(1)}, f32[32,24,128]{2,1,0:T(8,128)S(1)}) custom-call(s32[16,128]{1,0:T(8,128)S(1)} %get-tuple-element.10.ids, f32[4,8,4,8,128]{4,3,2,1,0:T(8,128)S(1)} %get-tuple-element.11.rows_out, f32[32,4,8,128]{3,2,1,0:T(8,128)S(1)} %get-tuple-element.12.column), custom_call_target="tpu_custom_call" | custom-call | tf_op jit(solution)/shard_map/pairs/pallas_call | solution.py:369
  31.8 18.2 %reduce.1 = f32[3,8,128]{2,1,0:T(8,128)S(1)} custom-call(f32[4,8,24,128]{3,2,1,0:T(8,128)S(1)} %get-tuple-element.13.row_force, f32[32,24,128]{2,1,0:T(8,128)S(1)} %get-tuple-element.14.column_force), custom_call_target="tpu_custom_call" | custom-call | tf_op jit(solution)/shard_map/reduce/pallas_call | solution.py:387
  50.0 0.6 %copy.7 = f32[8,3,128]{2,0,1:T(8,128)} copy(f32[8,3,128]{2,0,1:T(8,128)S(1)} %bitcast.2) | data formatting | bytes 24576

commit v6 on v5

--- a/solution.py
+++ b/solution.py
@@ -35,12 +35,13 @@
     return lax.axis_index("sink"), lax.axis_index("src")
 
 
-def greet(peers):
+def greet(peers, meanwhile):
     barrier = pltpu.get_barrier_semaphore()
     for peer in peers:
         pl.semaphore_signal(
             barrier, inc=1, device_id=peer, device_id_type=pl.DeviceIdType.MESH
         )
+    meanwhile()
     pl.semaphore_wait(barrier, len(peers))
 
 
@@ -59,10 +60,6 @@
     ring = chips // 2 - ring if back else ring
     within = lax.rem(lax.rem(sink, chips) // 2 + ring, chips // 2)
     return lax.rem(sink // chips + half, 2) * chips + within * 2 + lax.rem(sink, 2)
-
-
-def place_of(sink, chips):
-    return lax.rem(sink, 2) * chips + sink // 2
 
 
 def remote(source, target, send, recv, device):
@@ -76,9 +73,36 @@
     )
 
 
+def compact(group, core, ids, w):
+    a = jnp.concatenate([ids[w, 0:1, :], ids[w, 2:3, :]], axis=1)
+    b = jnp.concatenate([ids[w, 1:2, :], ids[w, 3:4, :]], axis=1)
+    count = jnp.concatenate([ids[w, 4:5, :], ids[w, 5:6, :]], axis=1)
+    owner = b // (LEAF_DEV * group)
+    slot = lax.broadcasted_iota(jnp.int32, (1, PAIR_CAP), 1)
+    chosen = (slot < count) & (owner % 2 == core)
+    flag = jnp.where(chosen, 1.0, 0.0)
+    sink = (w * group * LEAF_DEV + a % (group * LEAF_DEV)).astype(F32)
+    source = (owner // 2 * LEAF_DEV + b % LEAF_DEV).astype(F32)
+    row = lax.broadcasted_iota(jnp.int32, (PAIR_CAP, PAIR_CAP), 0)
+    lane = lax.broadcasted_iota(jnp.int32, (PAIR_CAP, PAIR_CAP), 1)
+    before = jnp.where(row < lane, 1.0, 0.0).astype(BF16)
+    flags = jnp.broadcast_to(flag, (16, PAIR_CAP)).astype(BF16)
+    order = jnp.dot(flags, before, preferred_element_type=F32)[0:1, :]
+    order = jnp.where(chosen, order, -1.0)
+    pick = jnp.where(row.astype(F32) == order, 1.0, 0.0).astype(BF16)
+    values = jnp.concatenate(
+        [jnp.broadcast_to(sink, (8, PAIR_CAP)), jnp.broadcast_to(source, (8, PAIR_CAP))], axis=0
+    ).astype(BF16)
+    packed = lax.dot_general(
+        values, pick, (((1,), (1,)), ((), ())), preferred_element_type=F32
+    ).astype(jnp.int32)
+    total = jnp.sum(flag, axis=1, keepdims=True).astype(jnp.int32)
+    return packed[0:1, :] * 128 + packed[8:9, :], total
+
+
 def gather_kernel(
     chips, group, pos, mass, ids, count, column_out, codes, rows_out,
-    ids_out, pack, ids_in, load, column_send, column_recv, row_send, row_recv, pass_send, pass_recv,
+    ids_out, pack, ids_in, load, column_send, column_recv, row_send, row_recv,
     hand_send, hand_recv, own_send, own_recv,
 ):
     sink, src, core, half, steps, rows = peers_of(chips, group)
@@ -99,13 +123,18 @@
     ]
     for copy in loads:
         copy.start()
-    greet(column + [peer for h, o, peer in row if o] + [partner, diagonal])
-    for copy in loads:
-        copy.wait()
     mine = core * 2 + half
-    ids_out[mine, 0:2, :] = ids_in[0, 0, :, 0:128]
-    ids_out[mine, 2:4, :] = ids_in[0, 0, :, 128:256]
-    ids_out[mine, 4:8, :] = jnp.full((4, CELLS), count[0, 0], jnp.int32)
+
+    def own_block():
+        for copy in loads:
+            copy.wait()
+        ids_out[mine, 0:2, :] = ids_in[0, 0, :, 0:128]
+        ids_out[mine, 2:4, :] = ids_in[0, 0, :, 128:256]
+        ids_out[mine, 4:8, :] = jnp.full((4, CELLS), count[0, 0], jnp.int32)
+        column_out[sink // 2] = pack[...]
+        rows_out[mine, src] = pack[...]
+
+    greet(column + [peer for h, o, peer in row if o] + [partner, diagonal], own_block)
 
     sends = []
 
@@ -114,61 +143,51 @@
         sends.append(copy)
 
     for i, peer in enumerate(column):
-        start(remote(pack, column_out.at[place_of(sink, chips)], column_send.at[i], column_recv.at[i], peer))
+        start(remote(pack, column_out.at[sink // 2], column_send.at[i], column_recv.at[i], peer))
     for i, (h, o, peer) in enumerate(row):
         start(remote(pack, rows_out.at[mine, src], row_send.at[i], row_recv.at[i], peer))
-    start(remote(pack, column_out.at[place_of(sink, chips)], own_send.at[0], own_recv.at[0], partner))
-    start(remote(pack, rows_out.at[mine, src], own_send.at[1], own_recv.at[1], partner))
+    start(remote(pack, rows_out.at[mine, src], own_send.at[0], own_recv.at[0], partner))
     pool = [partner, (across, src), diagonal]
     for i, peer in enumerate(pool):
-        start(remote(ids_out.at[mine], ids_out.at[mine], own_send.at[2 + i], own_recv.at[2 + i], peer))
-    column_out[place_of(sink, chips)] = pack[...]
-    rows_out[mine, src] = pack[...]
+        start(remote(ids_out.at[mine], ids_out.at[mine], own_send.at[1 + i], own_recv.at[1 + i], peer))
 
     for i, (h, o, peer) in reversed(list(enumerate(row))):
         block = rows_out.at[core * 2 + lax.rem(half + h, 2), lax.rem(src + group - o, group)]
         remote(pack, block, row_send.at[i], row_recv.at[i], partner).wait_recv()
         start(remote(block, block, hand_send.at[i], hand_recv.at[i], partner))
+
+    origins = [other * 2 + half, core * 2 + 1 - half, other * 2 + 1 - half]
+    for i, origin in enumerate(origins):
+        remote(ids_out.at[mine], ids_out.at[origin], own_send.at[1 + i], own_recv.at[1 + i], partner).wait_recv()
+    for w in range(4):
+        code, total = compact(group, core, ids_out, w)
+        codes[2 * w : 2 * w + 1, :] = code[:, 0:128]
+        codes[2 * w + 1 : 2 * w + 2, :] = code[:, 128:256]
+        codes[8 + w : 9 + w, :] = jnp.broadcast_to(total, (1, CELLS))
+    codes[12:16, :] = jnp.zeros((4, CELLS), jnp.int32)
+
     for i, step in reversed(list(enumerate(steps))):
-        block = column_out.at[place_of(moved(sink, chips, step, back=True), chips)]
+        block = column_out.at[moved(sink, chips, step, back=True) // 2]
         remote(pack, block, column_send.at[i], column_recv.at[i], partner).wait_recv()
-        start(remote(block, block, pass_send.at[i], pass_recv.at[i], partner))
-
+    remote(pack, rows_out.at[other * 2 + half, src], own_send.at[0], own_recv.at[0], partner).wait_recv()
     for i, (h, o, peer) in reversed(list(enumerate(row))):
         block = rows_out.at[other * 2 + lax.rem(half + h, 2), lax.rem(src + group - o, group)]
         remote(pack, block, hand_send.at[i], hand_recv.at[i], partner).wait_recv()
-    remote(pack, rows_out.at[other * 2 + half, src], own_send.at[1], own_recv.at[1], partner).wait_recv()
-    for i, step in reversed(list(enumerate(steps))):
-        block = column_out.at[place_of(moved(partner[0], chips, step, back=True), chips)]
-        remote(pack, block, pass_send.at[i], pass_recv.at[i], partner).wait_recv()
-    remote(pack, column_out.at[place_of(partner[0], chips)], own_send.at[0], own_recv.at[0], partner).wait_recv()
-    origins = [other * 2 + half, core * 2 + 1 - half, other * 2 + 1 - half]
-    for i, origin in enumerate(origins):
-        remote(ids_out.at[mine], ids_out.at[origin], own_send.at[2 + i], own_recv.at[2 + i], partner).wait_recv()
-    for w in range(4):
-        for h in range(2):
-            a = ids_out[w, 2 * h : 2 * h + 1, :]
-            b = ids_out[w, 2 * h + 1 : 2 * h + 2, :]
-            owner = b // (LEAF_DEV * group)
-            source = (owner % 2 * chips + owner // 2) * LEAF_DEV + b % LEAF_DEV
-            target = w * group * LEAF_DEV + a % (group * LEAF_DEV)
-            codes[2 * w + h : 2 * w + h + 1, :] = target * 256 + source
-        codes[8 + w : 9 + w, :] = ids_out[w, 4:5, :]
     for copy in sends:
         copy.wait_send()
 
 
 def pair_kernel(
-    chips, group, ids, rows_out, column, row_force, column_force, parts, choose, acc, first_x, second_x
+    chips, group, ids, rows_out, column, acc, column_force, parts, choose, first_x, second_x
 ):
     sink = lax.axis_index("sink")
-    mine = lax.rem(sink, 2) * 2 + sink // chips
+    half = sink // chips
     starts = [0]
     for w in range(4):
         starts.append(starts[w] + ids[8 + w, 0])
     every = starts[4]
-    begin = mine * every // 4
-    end = (mine + 1) * every // 4
+    begin = half * every // 2
+    end = (half + 1) * every // 2
     last = jnp.maximum(end - 1, 0)
     column_force[...] = jnp.zeros_like(column_force)
     depth = lax.broadcasted_iota(jnp.int32, (128, 512), 0)
@@ -193,7 +212,6 @@
             for h in range(group):
                 split(w, h)
 
-
     acc[...] = jnp.zeros_like(acc)
     lane = lax.broadcasted_iota(jnp.int32, (8, 128), 1)
 
@@ -208,16 +226,16 @@
     def fill(target, first):
         for u in range(UNROLL):
             code = look(first + u)
-            target[u] = jnp.dot(parts[code >> 11], choose[code >> 8 & 7], preferred_element_type=F32)
+            target[u] = jnp.dot(parts[code >> 10], choose[code >> 7 & 7], preferred_element_type=F32)
 
     def use(spread, first):
         done = []
         for u in range(UNROLL):
             code = look(first + u)
-            source_block = code >> 3 & 31
+            source_block = code >> 3 & 15
             source_k = code & 7
             live = jnp.where(first + u < end, FACTOR, 0.0)
-            at = (code >> 11 & 3) * 32 + (code >> 8 & 7)
+            at = (code >> 10 & 3) * 32 + (code >> 7 & 7)
             here = [
                 jnp.broadcast_to(column[source_block, c, pl.ds(source_k, 1), :], (8, 128))
                 for c in range(4)
@@ -243,7 +261,7 @@
                         jnp.where(masks[1], total[1], jnp.where(masks[2], total[2], 0.0)),
                     )
                 )
-            done.append((code >> 13, source_block, source_k, source_sum, sink_sum))
+            done.append((code >> 12, source_block, source_k, source_sum, sink_sum))
         for g, source_block, source_k, source_sum, sink_sum in done:
             for i, value in enumerate(sink_sum):
                 acc[g, pl.ds(8 * i, 8), :] += value
@@ -263,24 +281,11 @@
         return carry
 
     lax.fori_loop(0, (end - begin + 2 * UNROLL - 1) // (2 * UNROLL), turn, 0)
-    for w in range(4):
-        used = (starts[w] < end) & (starts[w + 1] > begin)
-
-        @pl.when(used)
-        def _(w=w):
-            for g in range(group // 4):
-                turned = acc[w * (group // 4) + g].T
-                for h in range(4):
-                    row_force[w, g * 4 + h] = turned[32 * h : 32 * h + FORCES, :]
-
-        @pl.when(jnp.logical_not(used))
-        def _(w=w):
-            row_force[w] = jnp.zeros_like(row_force[w])
 
 
 def reduce_kernel(
-    chips, group, row_force, column_force, out,
-    row_sum, column_sum, row_in, column_in, swap_row, swap_column,
+    chips, group, acc, column_force, out,
+    row_force, row_sum, row_in, column_in, swap_row,
     column_send, column_recv, row_send, row_recv, swap_send, swap_recv,
 ):
     sink, src, core, half, steps, rows = peers_of(chips, group)
@@ -292,22 +297,23 @@
         (h, o, (across if h else sink, lax.rem(src + o, group)))
         for o in rows for h in (1, 0) if (h, o) != (0, 0)
     ]
-    greet(column + [peer for h, o, peer in row if o] + [partner])
-    to_column = remote(
-        column_force.at[pl.ds(other * chips, chips)], swap_column,
-        swap_send.at[0], swap_recv.at[0], partner,
+
+    def turn_rows():
+        for g in range(group):
+            turned = acc[g].T
+            for h in range(4):
+                at = g * 4 + h
+                row_force[at // group, at % group] = turned[32 * h : 32 * h + FORCES, :]
+
+    greet(column + [peer for h, o, peer in row if o] + [partner], turn_rows)
+    to_row = remote(
+        row_force.at[pl.ds(other * 2, 2)], swap_row, swap_send.at[0], swap_recv.at[0], partner
     )
-    to_row = remote(
-        row_force.at[pl.ds(other * 2, 2)], swap_row, swap_send.at[1], swap_recv.at[1], partner
-    )
-    to_column.start()
     to_row.start()
-    to_column.wait_recv()
-    column_sum[...] = column_force[pl.ds(core * chips, chips)] + swap_column[...]
-    sends = [to_column, to_row]
+    sends = [to_row]
     for i, peer in enumerate(column):
         copy = remote(
-            column_sum.at[peer[0] // 2], column_in.at[i], column_send.at[i], column_recv.at[i], peer
+            column_force.at[peer[0] // 2], column_in.at[i], column_send.at[i], column_recv.at[i], peer
         )
         copy.start()
         sends.append(copy)
@@ -320,12 +326,12 @@
         )
         copy.start()
         sends.append(copy)
-    total = column_sum[sink // 2] + row_sum[half, src]
+    total = column_force[sink // 2] + row_sum[half, src]
     for i in reversed(range(len(row))):
         remote(row_sum.at[0, 0], row_in.at[i], row_send.at[i], row_recv.at[i], partner).wait_recv()
         total = total + row_in[i]
     for i in reversed(range(len(column))):
-        remote(column_sum.at[0], column_in.at[i], column_send.at[i], column_recv.at[i], partner).wait_recv()
+        remote(column_force.at[0], column_in.at[i], column_send.at[i], column_recv.at[i], partner).wait_recv()
         total = total + column_in[i]
     out[...] = total.reshape(3, LEAF_DEV, CELLS)
     for copy in sends:
@@ -341,7 +347,7 @@
         functools.partial(gather_kernel, chips, group),
         name="gather",
         out_shape=(
-            jax.ShapeDtypeStruct((2 * chips, 4, LEAF_DEV, CELLS), F32),
+            jax.ShapeDtypeStruct((chips, 4, LEAF_DEV, CELLS), F32),
             jax.ShapeDtypeStruct((16, CELLS), jnp.int32),
             jax.ShapeDtypeStruct((4, group, 4, LEAF_DEV, CELLS), F32),
         ),
@@ -354,9 +360,8 @@
             dma((3,)),
             dma((chips - 1,)), dma((chips - 1,)),
             dma((2 * group - 1,)), dma((2 * group - 1,)),
-            dma((chips - 1,)), dma((chips - 1,)),
             dma((2 * group - 1,)), dma((2 * group - 1,)),
-            dma((5,)), dma((5,)),
+            dma((4,)), dma((4,)),
         ],
         compiler_params=pltpu.CompilerParams(
             collective_id=0, has_side_effects=True, vmem_limit_bytes=16 << 20
@@ -366,19 +371,18 @@
         for x in (jnp.transpose(leaf_pos, (1, 0, 2)), leaf_mass, pair_ids)
     ), pair_count)
     blocks = 4 * group
-    row_force, column_force = pl.pallas_call(
+    acc, column_force = pl.pallas_call(
         functools.partial(pair_kernel, chips, group),
         name="pairs",
         out_shape=(
-            jax.ShapeDtypeStruct((4, group, FORCES, CELLS), F32),
-            jax.ShapeDtypeStruct((2 * chips, FORCES, CELLS), F32),
+            jax.ShapeDtypeStruct((blocks // 4, 128, 128), F32),
+            jax.ShapeDtypeStruct((chips, FORCES, CELLS), F32),
         ),
         in_specs=[smem, vmem, vmem],
         out_specs=(vmem, vmem),
         scratch_shapes=[
             pltpu.VMEM((4 * group, 128, 128), BF16),
             pltpu.VMEM((8, 128, 512), BF16),
-            pltpu.VMEM((blocks // 4, 128, 128), F32),
             pltpu.VMEM((UNROLL, 128, 512), F32),
             pltpu.VMEM((UNROLL, 128, 512), F32),
         ],
@@ -391,20 +395,19 @@
         in_specs=[vmem, vmem],
         out_specs=vmem,
         scratch_shapes=[
+            pltpu.VMEM((4, group, FORCES, CELLS), F32),
             pltpu.VMEM((2, group, FORCES, CELLS), F32),
-            pltpu.VMEM((chips, FORCES, CELLS), F32),
             pltpu.VMEM((2 * group - 1, FORCES, CELLS), F32),
             pltpu.VMEM((chips - 1, FORCES, CELLS), F32),
             pltpu.VMEM((2, group, FORCES, CELLS), F32),
-            pltpu.VMEM((chips, FORCES, CELLS), F32),
             dma((chips - 1,)), dma((chips - 1,)),
             dma((2 * group - 1,)), dma((2 * group - 1,)),
-            dma((2,)), dma((2,)),
+            dma((1,)), dma((1,)),
         ],
         compiler_params=pltpu.CompilerParams(
             collective_id=1, has_side_effects=True, vmem_limit_bytes=16 << 20
         ),
-    )(row_force, column_force)
+    )(acc, column_force)
     return jnp.transpose(force, (1, 0, 2))
 
 

time: 50.7 us -> 49.6 us (0.978)
  the two profiles are of different devices: /device:TPU:2 before, /device:TPU:1 now
where the time goes in v6:
time: 49.6 us; the launch traced here: 49.5 us
  Pallas kernels  48.2 us (97%)
  between operations  0.68 us (1%)
  local copies, waits for them, and re-layouts  0.6 us (1%)
    pallas_call x1, Pallas kernels, per_device(): pl.pallas_call(functools.partial(gather_kernel, chips, group), name='gath...  20.5 us
    pallas_call x1, Pallas kernels, per_device(): pl.pallas_call(functools.partial(pair_kernel, chips, group), name='pairs'...  16.1 us
    pallas_call x1, Pallas kernels, per_device(): pl.pallas_call(functools.partial(reduce_kernel, chips, group), name='redu...  11.6 us

profile of v6, /device:TPU:1, one launch (start us, length us, event | category | flops | bytes accessed | tf_op | source)
XLA Modules:
  0.0 49.5 jit_solution(12750749945986021732)
XLA Ops:
  0.7 20.5 %gather.1 = (f32[16,4,8,128]{3,2,1,0:T(8,128)S(1)}, s32[16,128]{1,0:T(8,128)S(1)}, f32[4,8,4,8,128]{4,3,2,1,0:T(8,128)S(1)}) custom-call(f32[3,8,128]{2,1,0:T(8,128)} %bitcast.3, f32[8,128]{1,0:T(8,128)} %mass.1, s32[1,1,2,256]{3,2,1,0:T(2,128)} %ids.1, s32[1,1]{1,0:T(1,128)S(6)} %copy.6.count), custom_call_target="tpu_custom_call" | custom-call | tf_op jit(solution)/shard_map/gather/pallas_call | solution.py:346
  21.2 16.1 %pairs.1 = (f32[8,128,128]{2,1,0:T(8,128)S(1)}, f32[16,24,128]{2,1,0:T(8,128)S(1)}) custom-call(s32[16,128]{1,0:T(8,128)S(1)} %get-tuple-element.10.ids, f32[4,8,4,8,128]{4,3,2,1,0:T(8,128)S(1)} %get-tuple-element.11.rows_out, f32[16,4,8,128]{3,2,1,0:T(8,128)S(1)} %get-tuple-element.12.column), custom_call_target="tpu_custom_call" | custom-call | tf_op jit(solution)/shard_map/pairs/pallas_call | solution.py:374
  37.3 11.6 %reduce.1 = f32[3,8,128]{2,1,0:T(8,128)S(1)} custom-call(f32[8,128,128]{2,1,0:T(8,128)S(1)} %get-tuple-element.13.acc, f32[16,24,128]{2,1,0:T(8,128)S(1)} %get-tuple-element.14.column_force), custom_call_target="tpu_custom_call" | custom-call | tf_op jit(solution)/shard_map/reduce/pallas_call | solution.py:391
  48.9 0.6 %copy.7 = f32[8,3,128]{2,0,1:T(8,128)} copy(f32[8,3,128]{2,0,1:T(8,128)S(1)} %bitcast.2) | data formatting | bytes 24576

commit v7 on v6

--- a/solution.py
+++ b/solution.py
@@ -49,17 +49,17 @@
     sink, src = place()
     core = lax.rem(sink, 2)
     half = sink // chips
-    rings = sorted(range(chips // 2), key=lambda o: -min(o, chips // 2 - o))
-    steps = [(h, o) for o in rings for h in (1, 0) if (h, o) != (0, 0)]
+    steps = sorted(range(1, chips // 2), key=lambda o: -min(o, chips // 2 - o))
     rows = sorted(range(group), key=lambda o: -min(o, group - o))
     return sink, src, core, half, steps, rows
 
 
-def moved(sink, chips, step, back=False):
-    half, ring = step
-    ring = chips // 2 - ring if back else ring
-    within = lax.rem(lax.rem(sink, chips) // 2 + ring, chips // 2)
-    return lax.rem(sink // chips + half, 2) * chips + within * 2 + lax.rem(sink, 2)
+def ringed(sink, chips, step):
+    return lax.rem(lax.rem(sink, chips) // 2 + step, chips // 2)
+
+
+def moved(sink, chips, step):
+    return sink // chips * chips + ringed(sink, chips, step) * 2 + lax.rem(sink, 2)
 
 
 def remote(source, target, send, recv, device):
@@ -73,16 +73,16 @@
     )
 
 
-def compact(group, core, ids, w):
+def compact(chips, group, core, half, ids, w):
     a = jnp.concatenate([ids[w, 0:1, :], ids[w, 2:3, :]], axis=1)
     b = jnp.concatenate([ids[w, 1:2, :], ids[w, 3:4, :]], axis=1)
     count = jnp.concatenate([ids[w, 4:5, :], ids[w, 5:6, :]], axis=1)
     owner = b // (LEAF_DEV * group)
     slot = lax.broadcasted_iota(jnp.int32, (1, PAIR_CAP), 1)
-    chosen = (slot < count) & (owner % 2 == core)
+    chosen = (slot < count) & (owner % 2 == core) & (owner // chips == half)
     flag = jnp.where(chosen, 1.0, 0.0)
     sink = (w * group * LEAF_DEV + a % (group * LEAF_DEV)).astype(F32)
-    source = (owner // 2 * LEAF_DEV + b % LEAF_DEV).astype(F32)
+    source = (owner % chips // 2 * LEAF_DEV + b % LEAF_DEV).astype(F32)
     row = lax.broadcasted_iota(jnp.int32, (PAIR_CAP, PAIR_CAP), 0)
     lane = lax.broadcasted_iota(jnp.int32, (PAIR_CAP, PAIR_CAP), 1)
     before = jnp.where(row < lane, 1.0, 0.0).astype(BF16)
@@ -97,7 +97,7 @@
         values, pick, (((1,), (1,)), ((), ())), preferred_element_type=F32
     ).astype(jnp.int32)
     total = jnp.sum(flag, axis=1, keepdims=True).astype(jnp.int32)
-    return packed[0:1, :] * 128 + packed[8:9, :], total
+    return packed[0:1, :] * 64 + packed[8:9, :], total
 
 
 def gather_kernel(
@@ -131,10 +131,10 @@
         ids_out[mine, 0:2, :] = ids_in[0, 0, :, 0:128]
         ids_out[mine, 2:4, :] = ids_in[0, 0, :, 128:256]
         ids_out[mine, 4:8, :] = jnp.full((4, CELLS), count[0, 0], jnp.int32)
-        column_out[sink // 2] = pack[...]
+        column_out[ringed(sink, chips, 0)] = pack[...]
         rows_out[mine, src] = pack[...]
 
-    greet(column + [peer for h, o, peer in row if o] + [partner, diagonal], own_block)
+    greet(column + [peer for h, o, peer in row] + [partner, diagonal], own_block)
 
     sends = []
 
@@ -143,7 +143,7 @@
         sends.append(copy)
 
     for i, peer in enumerate(column):
-        start(remote(pack, column_out.at[sink // 2], column_send.at[i], column_recv.at[i], peer))
+        start(remote(pack, column_out.at[ringed(sink, chips, 0)], column_send.at[i], column_recv.at[i], peer))
     for i, (h, o, peer) in enumerate(row):
         start(remote(pack, rows_out.at[mine, src], row_send.at[i], row_recv.at[i], peer))
     start(remote(pack, rows_out.at[mine, src], own_send.at[0], own_recv.at[0], partner))
@@ -160,14 +160,14 @@
     for i, origin in enumerate(origins):
         remote(ids_out.at[mine], ids_out.at[origin], own_send.at[1 + i], own_recv.at[1 + i], partner).wait_recv()
     for w in range(4):
-        code, total = compact(group, core, ids_out, w)
+        code, total = compact(chips, group, core, half, ids_out, w)
         codes[2 * w : 2 * w + 1, :] = code[:, 0:128]
         codes[2 * w + 1 : 2 * w + 2, :] = code[:, 128:256]
         codes[8 + w : 9 + w, :] = jnp.broadcast_to(total, (1, CELLS))
     codes[12:16, :] = jnp.zeros((4, CELLS), jnp.int32)
 
     for i, step in reversed(list(enumerate(steps))):
-        block = column_out.at[moved(sink, chips, step, back=True) // 2]
+        block = column_out.at[ringed(sink, chips, chips // 2 - step)]
         remote(pack, block, column_send.at[i], column_recv.at[i], partner).wait_recv()
     remote(pack, rows_out.at[other * 2 + half, src], own_send.at[0], own_recv.at[0], partner).wait_recv()
     for i, (h, o, peer) in reversed(list(enumerate(row))):
@@ -180,15 +180,11 @@
 def pair_kernel(
     chips, group, ids, rows_out, column, acc, column_force, parts, choose, first_x, second_x
 ):
-    sink = lax.axis_index("sink")
-    half = sink // chips
     starts = [0]
     for w in range(4):
         starts.append(starts[w] + ids[8 + w, 0])
     every = starts[4]
-    begin = half * every // 2
-    end = (half + 1) * every // 2
-    last = jnp.maximum(end - 1, 0)
+    last = jnp.maximum(every - 1, 0)
     column_force[...] = jnp.zeros_like(column_force)
     depth = lax.broadcasted_iota(jnp.int32, (128, 512), 0)
     field = lax.broadcasted_iota(jnp.int32, (128, 512), 1) // 128
@@ -207,7 +203,7 @@
 
     for w in range(4):
 
-        @pl.when((starts[w] < end) & (starts[w + 1] > begin))
+        @pl.when(starts[w] < starts[w + 1])
         def _(w=w):
             for h in range(group):
                 split(w, h)
@@ -226,16 +222,16 @@
     def fill(target, first):
         for u in range(UNROLL):
             code = look(first + u)
-            target[u] = jnp.dot(parts[code >> 10], choose[code >> 7 & 7], preferred_element_type=F32)
+            target[u] = jnp.dot(parts[code >> 9], choose[code >> 6 & 7], preferred_element_type=F32)
 
     def use(spread, first):
         done = []
         for u in range(UNROLL):
             code = look(first + u)
-            source_block = code >> 3 & 15
+            source_block = code >> 3 & 7
             source_k = code & 7
-            live = jnp.where(first + u < end, FACTOR, 0.0)
-            at = (code >> 10 & 3) * 32 + (code >> 7 & 7)
+            live = jnp.where(first + u < every, FACTOR, 0.0)
+            at = (code >> 9 & 3) * 32 + (code >> 6 & 7)
             here = [
                 jnp.broadcast_to(column[source_block, c, pl.ds(source_k, 1), :], (8, 128))
                 for c in range(4)
@@ -261,7 +257,7 @@
                         jnp.where(masks[1], total[1], jnp.where(masks[2], total[2], 0.0)),
                     )
                 )
-            done.append((code >> 12, source_block, source_k, source_sum, sink_sum))
+            done.append((code >> 11, source_block, source_k, source_sum, sink_sum))
         for g, source_block, source_k, source_sum, sink_sum in done:
             for i, value in enumerate(sink_sum):
                 acc[g, pl.ds(8 * i, 8), :] += value
@@ -270,17 +266,17 @@
                     source_sum[c], axis=0, keepdims=True
                 )
 
-    fill(first_x, begin)
+    fill(first_x, 0)
 
     def turn(i, carry):
-        first = begin + i * (2 * UNROLL)
+        first = i * (2 * UNROLL)
         fill(second_x, first + UNROLL)
         use(first_x, first)
         fill(first_x, first + 2 * UNROLL)
         use(second_x, first + UNROLL)
         return carry
 
-    lax.fori_loop(0, (end - begin + 2 * UNROLL - 1) // (2 * UNROLL), turn, 0)
+    lax.fori_loop(0, (every + 2 * UNROLL - 1) // (2 * UNROLL), turn, 0)
 
 
 def reduce_kernel(
@@ -305,7 +301,7 @@
                 at = g * 4 + h
                 row_force[at // group, at % group] = turned[32 * h : 32 * h + FORCES, :]
 
-    greet(column + [peer for h, o, peer in row if o] + [partner], turn_rows)
+    greet(column + [peer for h, o, peer in row] + [partner], turn_rows)
     to_row = remote(
         row_force.at[pl.ds(other * 2, 2)], swap_row, swap_send.at[0], swap_recv.at[0], partner
     )
@@ -313,7 +309,7 @@
     sends = [to_row]
     for i, peer in enumerate(column):
         copy = remote(
-            column_force.at[peer[0] // 2], column_in.at[i], column_send.at[i], column_recv.at[i], peer
+            column_force.at[ringed(sink, chips, steps[i])], column_in.at[i], column_send.at[i], column_recv.at[i], peer
         )
         copy.start()
         sends.append(copy)
@@ -326,7 +322,7 @@
         )
         copy.start()
         sends.append(copy)
-    total = column_force[sink // 2] + row_sum[half, src]
+    total = column_force[ringed(sink, chips, 0)] + row_sum[half, src]
     for i in reversed(range(len(row))):
         remote(row_sum.at[0, 0], row_in.at[i], row_send.at[i], row_recv.at[i], partner).wait_recv()
         total = total + row_in[i]
@@ -343,11 +339,12 @@
     smem = pl.BlockSpec(memory_space=pltpu.SMEM)
     hbm = pl.BlockSpec(memory_space=pltpu.HBM)
     dma = pltpu.SemaphoreType.DMA
+    ring = chips // 2
     column, codes, rows = pl.pallas_call(
         functools.partial(gather_kernel, chips, group),
         name="gather",
         out_shape=(
-            jax.ShapeDtypeStruct((chips, 4, LEAF_DEV, CELLS), F32),
+            jax.ShapeDtypeStruct((ring, 4, LEAF_DEV, CELLS), F32),
             jax.ShapeDtypeStruct((16, CELLS), jnp.int32),
             jax.ShapeDtypeStruct((4, group, 4, LEAF_DEV, CELLS), F32),
         ),
@@ -358,7 +355,7 @@
             pltpu.VMEM((4, LEAF_DEV, CELLS), F32),
             pltpu.VMEM((1, 1, 2, PAIR_CAP), jnp.int32),
             dma((3,)),
-            dma((chips - 1,)), dma((chips - 1,)),
+            dma((ring - 1,)), dma((ring - 1,)),
             dma((2 * group - 1,)), dma((2 * group - 1,)),
             dma((2 * group - 1,)), dma((2 * group - 1,)),
             dma((4,)), dma((4,)),
@@ -376,7 +373,7 @@
         name="pairs",
         out_shape=(
             jax.ShapeDtypeStruct((blocks // 4, 128, 128), F32),
-            jax.ShapeDtypeStruct((chips, FORCES, CELLS), F32),
+            jax.ShapeDtypeStruct((ring, FORCES, CELLS), F32),
         ),
         in_specs=[smem, vmem, vmem],
         out_specs=(vmem, vmem),
@@ -398,9 +395,9 @@
             pltpu.VMEM((4, group, FORCES, CELLS), F32),
             pltpu.VMEM((2, group, FORCES, CELLS), F32),
             pltpu.VMEM((2 * group - 1, FORCES, CELLS), F32),
-            pltpu.VMEM((chips - 1, FORCES, CELLS), F32),
+            pltpu.VMEM((ring - 1, FORCES, CELLS), F32),
             pltpu.VMEM((2, group, FORCES, CELLS), F32),
-            dma((chips - 1,)), dma((chips - 1,)),
+            dma((ring - 1,)), dma((ring - 1,)),
             dma((2 * group - 1,)), dma((2 * group - 1,)),
             dma((1,)), dma((1,)),
         ],

time: 49.6 us -> 43.8 us (0.88)
  Pallas kernels: 48.2 us -> 42.4 us
    pallas_call x1, Pallas kernels: 16.1 us -> 8.5 us  [per_device(): pl.pallas_call(functools.partial(pair_kernel, chips, group), name='pairs'...]
    pallas_call x1, Pallas kernels: 11.6 us -> 14.6 us  [per_device(): pl.pallas_call(functools.partial(reduce_kernel, chips, group), name='redu...]
    pallas_call x1, Pallas kernels: 20.5 us -> 19.3 us  [per_device(): pl.pallas_call(functools.partial(gather_kernel, chips, group), name='gath...]
where the time goes in v7:
time: 43.8 us; the launch traced here: 43.6 us
  Pallas kernels  42.4 us (97%)
  between operations  0.68 us (2%)
  local copies, waits for them, and re-layouts  0.6 us (1%)
    pallas_call x1, Pallas kernels, per_device(): pl.pallas_call(functools.partial(gather_kernel, chips, group), name='gath...  19.3 us
    pallas_call x1, Pallas kernels, per_device(): pl.pallas_call(functools.partial(reduce_kernel, chips, group), name='redu...  14.6 us
    pallas_call x1, Pallas kernels, per_device(): pl.pallas_call(functools.partial(pair_kernel, chips, group), name='pairs'...  8.5 us

profile of v7, /device:TPU:1, one launch (start us, length us, event | category | flops | bytes accessed | tf_op | source)
XLA Modules:
  0.0 43.6 jit_solution(17758731913555574198)
XLA Ops:
  0.7 19.3 %gather.1 = (f32[8,4,8,128]{3,2,1,0:T(8,128)S(1)}, s32[16,128]{1,0:T(8,128)S(1)}, f32[4,8,4,8,128]{4,3,2,1,0:T(8,128)S(1)}) custom-call(f32[3,8,128]{2,1,0:T(8,128)} %bitcast.3, f32[8,128]{1,0:T(8,128)} %mass.1, s32[1,1,2,256]{3,2,1,0:T(2,128)} %ids.1, s32[1,1]{1,0:T(1,128)S(6)} %copy.6.count), custom_call_target="tpu_custom_call" | custom-call | tf_op jit(solution)/shard_map/gather/pallas_call | solution.py:343
  19.9 8.5 %pairs.1 = (f32[8,128,128]{2,1,0:T(8,128)S(1)}, f32[8,24,128]{2,1,0:T(8,128)S(1)}) custom-call(s32[16,128]{1,0:T(8,128)S(1)} %get-tuple-element.10.ids, f32[4,8,4,8,128]{4,3,2,1,0:T(8,128)S(1)} %get-tuple-element.11.rows_out, f32[8,4,8,128]{3,2,1,0:T(8,128)S(1)} %get-tuple-element.12.column), custom_call_target="tpu_custom_call" | custom-call | tf_op jit(solution)/shard_map/pairs/pallas_call | solution.py:371
  28.4 14.6 %reduce.1 = f32[3,8,128]{2,1,0:T(8,128)S(1)} custom-call(f32[8,128,128]{2,1,0:T(8,128)S(1)} %get-tuple-element.13.acc, f32[8,24,128]{2,1,0:T(8,128)S(1)} %get-tuple-element.14.column_force), custom_call_target="tpu_custom_call" | custom-call | tf_op jit(solution)/shard_map/reduce/pallas_call | solution.py:388
  43.0 0.6 %copy.7 = f32[8,3,128]{2,0,1:T(8,128)} copy(f32[8,3,128]{2,0,1:T(8,128)S(1)} %bitcast.2) | data formatting | bytes 24576

commit v8 on v7

--- a/solution.py
+++ b/solution.py
@@ -101,7 +101,7 @@
 
 
 def gather_kernel(
-    chips, group, pos, mass, ids, count, column_out, codes, rows_out,
+    chips, group, pos, mass, ids, count, column_out, codes, rows_out, choose,
     ids_out, pack, ids_in, load, column_send, column_recv, row_send, row_recv,
     hand_send, hand_recv, own_send, own_recv,
 ):
@@ -133,6 +133,11 @@
         ids_out[mine, 4:8, :] = jnp.full((4, CELLS), count[0, 0], jnp.int32)
         column_out[ringed(sink, chips, 0)] = pack[...]
         rows_out[mine, src] = pack[...]
+        depth = lax.broadcasted_iota(jnp.int32, (96, 512), 0)
+        field = lax.broadcasted_iota(jnp.int32, (96, 512), 1) // 128
+        for k in range(8):
+            hit = (depth % 32 // 8 == field) & (depth % 8 == k)
+            choose[k] = jnp.where(hit, 1.0, 0.0).astype(BF16)
 
     greet(column + [peer for h, o, peer in row] + [partner, diagonal], own_block)
 
@@ -177,39 +182,38 @@
         copy.wait_send()
 
 
+def thirds(block):
+    high = block.astype(BF16).astype(F32)
+    rest = block - high
+    middle = rest.astype(BF16).astype(F32)
+    return high, middle, rest - middle
+
+
 def pair_kernel(
-    chips, group, ids, rows_out, column, acc, column_force, parts, choose, first_x, second_x
+    group, ring, ids, rows, column, choose, row_force, acc, parts, lines, first_x, second_x
 ):
     starts = [0]
     for w in range(4):
         starts.append(starts[w] + ids[8 + w, 0])
     every = starts[4]
     last = jnp.maximum(every - 1, 0)
-    column_force[...] = jnp.zeros_like(column_force)
-    depth = lax.broadcasted_iota(jnp.int32, (128, 512), 0)
-    field = lax.broadcasted_iota(jnp.int32, (128, 512), 1) // 128
-    hit = (depth < 96) & (depth % 32 // 8 == field)
-    for k in range(8):
-        choose[k] = jnp.where(hit & (depth % 8 == k), 1.0, 0.0).astype(BF16)
-
-    def split(line, at):
-        block = rows_out[line, at].reshape(FIELDS, CELLS)
-        high = block.astype(BF16).astype(F32)
-        rest = block - high
-        middle = rest.astype(BF16).astype(F32)
-        low = rest - middle
-        stacked = jnp.concatenate([high, middle, low, jnp.zeros_like(high)], axis=0)
-        parts[line * group + at] = stacked.T.astype(BF16)
-
+    row_force[...] = jnp.zeros_like(row_force)
+    acc[...] = jnp.zeros_like(acc)
+
+    for h in range(ring):
+        block = column[h].reshape(FIELDS, CELLS)
+        stacked = jnp.concatenate([*thirds(block), jnp.ones_like(block)], axis=0)
+        parts[h] = stacked.T.astype(BF16)
     for w in range(4):
 
         @pl.when(starts[w] < starts[w + 1])
         def _(w=w):
             for h in range(group):
-                split(w, h)
-
-    acc[...] = jnp.zeros_like(acc)
-    lane = lax.broadcasted_iota(jnp.int32, (8, 128), 1)
+                for i, third in enumerate(thirds(-rows[w, h, 0:3])):
+                    lines[i, w * group + h] = third
+
+    sub = lax.broadcasted_iota(jnp.int32, (8, CELLS), 0)
+    lane = lax.broadcasted_iota(jnp.int32, (8, CELLS), 1)
 
     def look(slot):
         slot = jnp.minimum(slot, last)
@@ -222,48 +226,61 @@
     def fill(target, first):
         for u in range(UNROLL):
             code = look(first + u)
-            target[u] = jnp.dot(parts[code >> 9], choose[code >> 6 & 7], preferred_element_type=F32)
+            sink_block, k = code >> 9, code >> 6 & 7
+            tops = []
+            for c in range(3):
+                high, middle, low = (
+                    jnp.broadcast_to(lines[i, sink_block, c, pl.ds(k, 1), :], (8, CELLS))
+                    for i in range(3)
+                )
+                tops.append(
+                    jnp.where(
+                        sub == 0, high, jnp.where(sub == 1, middle, jnp.where(sub == 2, low, 0.0))
+                    )
+                )
+            top = jnp.concatenate(tops + [jnp.zeros((8, CELLS), F32)], axis=1)
+            under = jnp.concatenate([top, jnp.zeros((8, 512), F32)], axis=0).astype(BF16)
+            rhs = jnp.concatenate([choose[code & 7], under, jnp.zeros((16, 512), BF16)], axis=0)
+            target[u] = jnp.dot(parts[code >> 3 & 7], rhs, preferred_element_type=F32)
 
     def use(spread, first):
         done = []
         for u in range(UNROLL):
             code = look(first + u)
-            source_block = code >> 3 & 7
-            source_k = code & 7
+            sink_block, k = code >> 9, code >> 6 & 7
             live = jnp.where(first + u < every, FACTOR, 0.0)
-            at = (code >> 9 & 3) * 32 + (code >> 6 & 7)
-            here = [
-                jnp.broadcast_to(column[source_block, c, pl.ds(source_k, 1), :], (8, 128))
-                for c in range(4)
-            ]
-            mass = here[3] * live
+            at = (code >> 3 & 3) * 32 + (code & 7)
+            sink_mass = jnp.broadcast_to(
+                rows[sink_block // group, sink_block % group, 3, pl.ds(k, 1), :], (8, CELLS)
+            )
+            mass = sink_mass * live
             masks = [lane == at + 8 * c for c in range(3)]
-            source_sum = [jnp.zeros((8, 128), F32) for _ in range(3)]
-            sink_sum = []
+            sink_sum = [jnp.zeros((8, CELLS), F32) for _ in range(3)]
+            source_sum = []
             for i in range(0, CELLS, 8):
-                there = [spread[u, i : i + 8, 128 * c : 128 * c + 128] for c in range(4)]
-                offset = [here[c] - there[c] for c in range(3)]
+                offset = [spread[u, i : i + 8, 128 * c : 128 * c + 128] for c in range(3)]
+                source_mass = spread[u, i : i + 8, 384:512]
                 dist_sq = (offset[0] * offset[0] + offset[1] * offset[1]) + (
                     offset[2] * offset[2] + SOFTEN
                 )
-                weight = (pair_weight(dist_sq) * there[3]) * mass
+                weight = (pair_weight(dist_sq) * source_mass) * mass
                 force = [weight * offset[c] for c in range(3)]
-                source_sum = [source_sum[c] + force[c] for c in range(3)]
+                sink_sum = [sink_sum[c] + force[c] for c in range(3)]
                 total = [jnp.sum(force[c], axis=1, keepdims=True) for c in range(3)]
-                sink_sum.append(
+                source_sum.append(
                     jnp.where(
                         masks[0],
                         total[0],
                         jnp.where(masks[1], total[1], jnp.where(masks[2], total[2], 0.0)),
                     )
                 )
-            done.append((code >> 11, source_block, source_k, source_sum, sink_sum))
-        for g, source_block, source_k, source_sum, sink_sum in done:
-            for i, value in enumerate(sink_sum):
-                acc[g, pl.ds(8 * i, 8), :] += value
+            done.append((code >> 5 & 1, sink_block, k, sink_sum, source_sum))
+        for g, sink_block, k, sink_sum, source_sum in done:
+            for i, value in enumerate(source_sum):
+                acc[g, pl.ds(8 * i, 8), :] -= value
             for c in range(3):
-                column_force[source_block, pl.ds(8 * c + source_k, 1), :] -= jnp.sum(
-                    source_sum[c], axis=0, keepdims=True
+                row_force[sink_block, pl.ds(8 * c + k, 1), :] += jnp.sum(
+                    sink_sum[c], axis=0, keepdims=True
                 )
 
     fill(first_x, 0)
@@ -280,8 +297,8 @@
 
 
 def reduce_kernel(
-    chips, group, acc, column_force, out,
-    row_force, row_sum, row_in, column_in, swap_row,
+    chips, group, row_force, acc, out,
+    column_force, row_sum, row_in, column_in, swap_row,
     column_send, column_recv, row_send, row_recv, swap_send, swap_recv,
 ):
     sink, src, core, half, steps, rows = peers_of(chips, group)
@@ -294,16 +311,15 @@
         for o in rows for h in (1, 0) if (h, o) != (0, 0)
     ]
 
-    def turn_rows():
-        for g in range(group):
+    def turn_column():
+        for g in range(chips // 8):
             turned = acc[g].T
             for h in range(4):
-                at = g * 4 + h
-                row_force[at // group, at % group] = turned[32 * h : 32 * h + FORCES, :]
-
-    greet(column + [peer for h, o, peer in row] + [partner], turn_rows)
+                column_force[g * 4 + h] = turned[32 * h : 32 * h + FORCES, :]
+
+    greet(column + [peer for h, o, peer in row] + [partner], turn_column)
     to_row = remote(
-        row_force.at[pl.ds(other * 2, 2)], swap_row, swap_send.at[0], swap_recv.at[0], partner
+        row_force.at[pl.ds(other * 2 * group, 2 * group)], swap_row, swap_send.at[0], swap_recv.at[0], partner
     )
     to_row.start()
     sends = [to_row]
@@ -314,17 +330,17 @@
         copy.start()
         sends.append(copy)
     to_row.wait_recv()
-    row_sum[...] = row_force[pl.ds(core * 2, 2)] + swap_row[...]
+    row_sum[...] = row_force[pl.ds(core * 2 * group, 2 * group)] + swap_row[...]
     for i, (h, o, peer) in enumerate(row):
         copy = remote(
-            row_sum.at[lax.rem(half + h, 2), peer[1]], row_in.at[i],
+            row_sum.at[lax.rem(half + h, 2) * group + peer[1]], row_in.at[i],
             row_send.at[i], row_recv.at[i], peer,
         )
         copy.start()
         sends.append(copy)
-    total = column_force[ringed(sink, chips, 0)] + row_sum[half, src]
+    total = column_force[ringed(sink, chips, 0)] + row_sum[half * group + src]
     for i in reversed(range(len(row))):
-        remote(row_sum.at[0, 0], row_in.at[i], row_send.at[i], row_recv.at[i], partner).wait_recv()
+        remote(row_sum.at[0], row_in.at[i], row_send.at[i], row_recv.at[i], partner).wait_recv()
         total = total + row_in[i]
     for i in reversed(range(len(column))):
         remote(column_force.at[0], column_in.at[i], column_send.at[i], column_recv.at[i], partner).wait_recv()
@@ -340,16 +356,17 @@
     hbm = pl.BlockSpec(memory_space=pltpu.HBM)
     dma = pltpu.SemaphoreType.DMA
     ring = chips // 2
-    column, codes, rows = pl.pallas_call(
+    column, codes, rows, choose = pl.pallas_call(
         functools.partial(gather_kernel, chips, group),
         name="gather",
         out_shape=(
             jax.ShapeDtypeStruct((ring, 4, LEAF_DEV, CELLS), F32),
             jax.ShapeDtypeStruct((16, CELLS), jnp.int32),
             jax.ShapeDtypeStruct((4, group, 4, LEAF_DEV, CELLS), F32),
+            jax.ShapeDtypeStruct((8, 96, 512), BF16),
         ),
         in_specs=[hbm] * 3 + [smem],
-        out_specs=(vmem,) * 3,
+        out_specs=(vmem,) * 4,
         scratch_shapes=[
             pltpu.VMEM((4, 8, CELLS), jnp.int32),
             pltpu.VMEM((4, LEAF_DEV, CELLS), F32),
@@ -367,24 +384,23 @@
         pltpu.with_memory_space_constraint(x, pltpu.HBM)
         for x in (jnp.transpose(leaf_pos, (1, 0, 2)), leaf_mass, pair_ids)
     ), pair_count)
-    blocks = 4 * group
-    acc, column_force = pl.pallas_call(
-        functools.partial(pair_kernel, chips, group),
+    row_force, acc = pl.pallas_call(
+        functools.partial(pair_kernel, group, ring),
         name="pairs",
         out_shape=(
-            jax.ShapeDtypeStruct((blocks // 4, 128, 128), F32),
-            jax.ShapeDtypeStruct((ring, FORCES, CELLS), F32),
+            jax.ShapeDtypeStruct((4 * group, FORCES, CELLS), F32),
+            jax.ShapeDtypeStruct((ring // 4, 128, CELLS), F32),
         ),
-        in_specs=[smem, vmem, vmem],
+        in_specs=[smem, vmem, vmem, vmem],
         out_specs=(vmem, vmem),
         scratch_shapes=[
-            pltpu.VMEM((4 * group, 128, 128), BF16),
-            pltpu.VMEM((8, 128, 512), BF16),
+            pltpu.VMEM((ring, 128, 128), BF16),
+            pltpu.VMEM((3, 4 * group, 3, LEAF_DEV, CELLS), F32),
             pltpu.VMEM((UNROLL, 128, 512), F32),
             pltpu.VMEM((UNROLL, 128, 512), F32),
         ],
         compiler_params=pltpu.CompilerParams(vmem_limit_bytes=40 << 20),
-    )(codes, rows, column)
+    )(codes, rows, column, choose)
     force = pl.pallas_call(
         functools.partial(reduce_kernel, chips, group),
         name="reduce",
@@ -392,11 +408,11 @@
         in_specs=[vmem, vmem],
         out_specs=vmem,
         scratch_shapes=[
-            pltpu.VMEM((4, group, FORCES, CELLS), F32),
-            pltpu.VMEM((2, group, FORCES, CELLS), F32),
+            pltpu.VMEM((ring, FORCES, CELLS), F32),
+            pltpu.VMEM((2 * group, FORCES, CELLS), F32),
             pltpu.VMEM((2 * group - 1, FORCES, CELLS), F32),
             pltpu.VMEM((ring - 1, FORCES, CELLS), F32),
-            pltpu.VMEM((2, group, FORCES, CELLS), F32),
+            pltpu.VMEM((2 * group, FORCES, CELLS), F32),
             dma((ring - 1,)), dma((ring - 1,)),
             dma((2 * group - 1,)), dma((2 * group - 1,)),
             dma((1,)), dma((1,)),
@@ -404,7 +420,7 @@
         compiler_params=pltpu.CompilerParams(
             collective_id=1, has_side_effects=True, vmem_limit_bytes=16 << 20
         ),
-    )(acc, column_force)
+    )(row_force, acc)
     return jnp.transpose(force, (1, 0, 2))
 
 

time: 43.8 us -> 43.1 us (0.984)
  Pallas kernels: 42.4 us -> 41.7 us
    pallas_call x1, Pallas kernels: 14.6 us -> 14.1 us  [per_device(): pl.pallas_call(functools.partial(reduce_kernel, chips, group), name='redu...]
where the time goes in v8:
time: 43.1 us; the launch traced here: 43 us
  Pallas kernels  41.7 us (97%)
  between operations  0.68 us (2%)
  local copies, waits for them, and re-layouts  0.6 us (1%)
    pallas_call x1, Pallas kernels, per_device(): pl.pallas_call(functools.partial(gather_kernel, chips, group), name='gath...  19.3 us
    pallas_call x1, Pallas kernels, per_device(): pl.pallas_call(functools.partial(reduce_kernel, chips, group), name='redu...  14.1 us
    pallas_call x1, Pallas kernels, per_device(): pl.pallas_call(functools.partial(pair_kernel, group, ring), name='pairs',...  8.38 us

profile of v8, /device:TPU:1, one launch (start us, length us, event | category | flops | bytes accessed | tf_op | source)
XLA Modules:
  0.0 43.0 jit_solution(2478216574634457701)
XLA Ops:
  0.7 19.3 %gather.1 = (f32[8,4,8,128]{3,2,1,0:T(8,128)S(1)}, s32[16,128]{1,0:T(8,128)S(1)}, f32[4,8,4,8,128]{4,3,2,1,0:T(8,128)S(1)}, bf16[8,96,512]{2,1,0:T(8,128)(2,1)S(1)}) custom-call(f32[3,8,128]{2,1,0:T(8,128)} %bitcast.3, f32[8,128]{1,0:T(8,128)} %mass.1, s32[1,1,2,256]{3,2,1,0:T(2,128)} %ids.1, s32[1,1]{1,0:T(1,128)S(6)} %copy.6.count), custom_call_target="tpu_custom_call" | custom-call | tf_op jit(solution)/shard_map/gather/pallas_call | solution.py:359
  19.9 8.4 %pairs.1 = (f32[32,24,128]{2,1,0:T(8,128)S(1)}, f32[2,128,128]{2,1,0:T(8,128)S(1)}) custom-call(s32[16,128]{1,0:T(8,128)S(1)} %get-tuple-element.11.ids, f32[4,8,4,8,128]{4,3,2,1,0:T(8,128)S(1)} %get-tuple-element.12.rows, f32[8,4,8,128]{3,2,1,0:T(8,128)S(1)} %get-tuple-element.13.column, bf16[8,96,512]{2,1,0:T(8,128)(2,1)S(1)} %get-tuple-element.14.choose), custom_call_target="tpu_custom_call" | custom-call | tf_op jit(solution)/shard_map/pairs/pallas_call | solution.py:387
  28.3 14.1 %reduce.1 = f32[3,8,128]{2,1,0:T(8,128)S(1)} custom-call(f32[32,24,128]{2,1,0:T(8,128)S(1)} %get-tuple-element.15.row_force, f32[2,128,128]{2,1,0:T(8,128)S(1)} %get-tuple-element.16.acc), custom_call_target="tpu_custom_call" | custom-call | tf_op jit(solution)/shard_map/reduce/pallas_call | solution.py:404
  42.4 0.6 %copy.7 = f32[8,3,128]{2,0,1:T(8,128)} copy(f32[8,3,128]{2,0,1:T(8,128)S(1)} %bitcast.2) | data formatting | bytes 24576

commit v9 on v8

--- a/solution.py
+++ b/solution.py
@@ -139,7 +139,7 @@
             hit = (depth % 32 // 8 == field) & (depth % 8 == k)
             choose[k] = jnp.where(hit, 1.0, 0.0).astype(BF16)
 
-    greet(column + [peer for h, o, peer in row] + [partner, diagonal], own_block)
+    greet([peer for h, o, peer in row] + column + [diagonal, partner], own_block)
 
     sends = []
 
@@ -147,16 +147,16 @@
         copy.start()
         sends.append(copy)
 
-    for i, peer in enumerate(column):
-        start(remote(pack, column_out.at[ringed(sink, chips, 0)], column_send.at[i], column_recv.at[i], peer))
     for i, (h, o, peer) in enumerate(row):
         start(remote(pack, rows_out.at[mine, src], row_send.at[i], row_recv.at[i], peer))
     start(remote(pack, rows_out.at[mine, src], own_send.at[0], own_recv.at[0], partner))
     pool = [partner, (across, src), diagonal]
     for i, peer in enumerate(pool):
         start(remote(ids_out.at[mine], ids_out.at[mine], own_send.at[1 + i], own_recv.at[1 + i], peer))
-
-    for i, (h, o, peer) in reversed(list(enumerate(row))):
+    for i, peer in enumerate(column):
+        start(remote(pack, column_out.at[ringed(sink, chips, 0)], column_send.at[i], column_recv.at[i], peer))
+
+    for i, (h, o, peer) in enumerate(row):
         block = rows_out.at[core * 2 + lax.rem(half + h, 2), lax.rem(src + group - o, group)]
         remote(pack, block, row_send.at[i], row_recv.at[i], partner).wait_recv()
         start(remote(block, block, hand_send.at[i], hand_recv.at[i], partner))
@@ -241,7 +241,8 @@
             top = jnp.concatenate(tops + [jnp.zeros((8, CELLS), F32)], axis=1)
             under = jnp.concatenate([top, jnp.zeros((8, 512), F32)], axis=0).astype(BF16)
             rhs = jnp.concatenate([choose[code & 7], under, jnp.zeros((16, 512), BF16)], axis=0)
-            target[u] = jnp.dot(parts[code >> 3 & 7], rhs, preferred_element_type=F32)
+            for n in (0, 256):
+                target[u, :, n : n + 256] = jnp.dot(parts[code >> 3 & 7], rhs[:, n : n + 256], preferred_element_type=F32)
 
     def use(spread, first):
         done = []
@@ -284,16 +285,27 @@
                 )
 
     fill(first_x, 0)
+    fill(second_x, UNROLL)
 
     def turn(i, carry):
         first = i * (2 * UNROLL)
-        fill(second_x, first + UNROLL)
         use(first_x, first)
         fill(first_x, first + 2 * UNROLL)
         use(second_x, first + UNROLL)
+        fill(second_x, first + 3 * UNROLL)
         return carry
 
-    lax.fori_loop(0, (every + 2 * UNROLL - 1) // (2 * UNROLL), turn, 0)
+    turns = every // (2 * UNROLL)
+    lax.fori_loop(0, turns, turn, 0)
+    done = turns * (2 * UNROLL)
+
+    @pl.when(done < every)
+    def _():
+        use(first_x, done)
+
+    @pl.when(done + UNROLL < every)
+    def _():
+        use(second_x, done + UNROLL)
 
 
 def reduce_kernel(
@@ -317,28 +329,34 @@
             for h in range(4):
                 column_force[g * 4 + h] = turned[32 * h : 32 * h + FORCES, :]
 
-    greet(column + [peer for h, o, peer in row] + [partner], turn_column)
-    to_row = remote(
-        row_force.at[pl.ds(other * 2 * group, 2 * group)], swap_row, swap_send.at[0], swap_recv.at[0], partner
-    )
-    to_row.start()
-    sends = [to_row]
+    greet([peer for h, o, peer in row] + column + [partner], turn_column)
+    order = [(h, o) for h, o, peer in row] + [(0, 0)]
+    blocks = [(lax.rem(half + h, 2) * group, lax.rem(src + o, group)) for h, o in order]
+    swaps = [
+        remote(
+            row_force.at[other * 2 * group + line + at], swap_row.at[i],
+            swap_send.at[i], swap_recv.at[i], partner,
+        )
+        for i, (line, at) in enumerate(blocks)
+    ]
+    sends = list(swaps)
+    for copy in swaps:
+        copy.start()
     for i, peer in enumerate(column):
         copy = remote(
-            column_force.at[ringed(sink, chips, steps[i])], column_in.at[i], column_send.at[i], column_recv.at[i], peer
+            column_force.at[ringed(sink, chips, steps[i])], column_in.at[i],
+            column_send.at[i], column_recv.at[i], peer,
         )
         copy.start()
         sends.append(copy)
-    to_row.wait_recv()
-    row_sum[...] = row_force[pl.ds(core * 2 * group, 2 * group)] + swap_row[...]
-    for i, (h, o, peer) in enumerate(row):
-        copy = remote(
-            row_sum.at[lax.rem(half + h, 2) * group + peer[1]], row_in.at[i],
-            row_send.at[i], row_recv.at[i], peer,
-        )
-        copy.start()
-        sends.append(copy)
-    total = column_force[ringed(sink, chips, 0)] + row_sum[half * group + src]
+    for i, (line, at) in enumerate(blocks):
+        swaps[i].wait_recv()
+        row_sum[i] = row_force[core * 2 * group + line + at] + swap_row[i]
+        if i < len(row):
+            copy = remote(row_sum.at[i], row_in.at[i], row_send.at[i], row_recv.at[i], row[i][2])
+            copy.start()
+            sends.append(copy)
+    total = column_force[ringed(sink, chips, 0)] + row_sum[len(row)]
     for i in reversed(range(len(row))):
         remote(row_sum.at[0], row_in.at[i], row_send.at[i], row_recv.at[i], partner).wait_recv()
         total = total + row_in[i]
@@ -415,7 +433,7 @@
             pltpu.VMEM((2 * group, FORCES, CELLS), F32),
             dma((ring - 1,)), dma((ring - 1,)),
             dma((2 * group - 1,)), dma((2 * group - 1,)),
-            dma((1,)), dma((1,)),
+            dma((2 * group,)), dma((2 * group,)),
         ],
         compiler_params=pltpu.CompilerParams(
             collective_id=1, has_side_effects=True, vmem_limit_bytes=16 << 20

time: 43.1 us -> 43.6 us (1.012); the launches traced: 43 us -> 42.7 us
    pallas_call x1, Pallas kernels: 8.38 us -> 5.74 us  [per_device(): pl.pallas_call(functools.partial(pair_kernel, group, ring), name='pairs',...]
    pallas_call x1, Pallas kernels: 14.1 us -> 16.5 us  [per_device(): pl.pallas_call(functools.partial(reduce_kernel, chips, group), name='redu...]
where the time goes in v9:
time: 43.6 us; the launch traced here: 42.7 us
  Pallas kernels  41.5 us (95%)
  between operations  0.68 us (2%)
  local copies, waits for them, and re-layouts  0.6 us (1%)
    pallas_call x1, Pallas kernels, per_device(): pl.pallas_call(functools.partial(gather_kernel, chips, group), name='gath...  19.2 us
    pallas_call x1, Pallas kernels, per_device(): pl.pallas_call(functools.partial(reduce_kernel, chips, group), name='redu...  16.5 us
    pallas_call x1, Pallas kernels, per_device(): pl.pallas_call(functools.partial(pair_kernel, group, ring), name='pairs',...  5.74 us

profile of v9, /device:TPU:1, one launch (start us, length us, event | category | flops | bytes accessed | tf_op | source)
XLA Modules:
  0.0 42.7 jit_solution(11279985551723661671)
XLA Ops:
  0.7 19.2 %gather.1 = (f32[8,4,8,128]{3,2,1,0:T(8,128)S(1)}, s32[16,128]{1,0:T(8,128)S(1)}, f32[4,8,4,8,128]{4,3,2,1,0:T(8,128)S(1)}, bf16[8,96,512]{2,1,0:T(8,128)(2,1)S(1)}) custom-call(f32[3,8,128]{2,1,0:T(8,128)} %bitcast.3, f32[8,128]{1,0:T(8,128)} %mass.1, s32[1,1,2,256]{3,2,1,0:T(2,128)} %ids.1, s32[1,1]{1,0:T(1,128)S(6)} %copy.6.count), custom_call_target="tpu_custom_call" | custom-call | tf_op jit(solution)/shard_map/gather/pallas_call | solution.py:377
  19.9 5.7 %pairs.1 = (f32[32,24,128]{2,1,0:T(8,128)S(1)}, f32[2,128,128]{2,1,0:T(8,128)S(1)}) custom-call(s32[16,128]{1,0:T(8,128)S(1)} %get-tuple-element.11.ids, f32[4,8,4,8,128]{4,3,2,1,0:T(8,128)S(1)} %get-tuple-element.12.rows, f32[8,4,8,128]{3,2,1,0:T(8,128)S(1)} %get-tuple-element.13.column, bf16[8,96,512]{2,1,0:T(8,128)(2,1)S(1)} %get-tuple-element.14.choose), custom_call_target="tpu_custom_call" | custom-call | tf_op jit(solution)/shard_map/pairs/pallas_call | solution.py:405
  25.6 16.5 %reduce.1 = f32[3,8,128]{2,1,0:T(8,128)S(1)} custom-call(f32[32,24,128]{2,1,0:T(8,128)S(1)} %get-tuple-element.15.row_force, f32[2,128,128]{2,1,0:T(8,128)S(1)} %get-tuple-element.16.acc), custom_call_target="tpu_custom_call" | custom-call | tf_op jit(solution)/shard_map/reduce/pallas_call | solution.py:422
  42.1 0.6 %copy.7 = f32[8,3,128]{2,0,1:T(8,128)} copy(f32[8,3,128]{2,0,1:T(8,128)S(1)} %bitcast.2) | data formatting | bytes 24576

commit v10 on v9

--- a/solution.py
+++ b/solution.py
@@ -27,8 +27,8 @@
     square = dist_sq * FALLOFF
     inverse = lax.rsqrt(square)
     tail = 1.0 - lax.erf(square * inverse)
-    bell = jnp.exp2(dist_sq * (-FALLOFF / math.log(2.0)))
-    return (tail * inverse + bell * TWO_ROOT_PI) * (inverse * inverse)
+    bell = jnp.exp2(dist_sq * (-FALLOFF / math.log(2.0)) + math.log2(TWO_ROOT_PI))
+    return (tail * inverse + bell) * (inverse * inverse)
 
 
 def place():

time: 43.6 us -> 43.7 us (level); the launches traced: 42.7 us -> 43.6 us
  Pallas kernels: 41.5 us -> 42.3 us
    pallas_call x1, Pallas kernels: 5.74 us -> 7.65 us  [per_device(): pl.pallas_call(functools.partial(pair_kernel, group, ring), name='pairs',...]
    pallas_call x1, Pallas kernels: 16.5 us -> 15.5 us  [per_device(): pl.pallas_call(functools.partial(reduce_kernel, chips, group), name='redu...]
where the time goes in v10:
time: 43.7 us; the launch traced here: 43.6 us
  Pallas kernels  42.3 us (97%)
  between operations  0.67 us (2%)
  local copies, waits for them, and re-layouts  0.6 us (1%)
    pallas_call x1, Pallas kernels, per_device(): pl.pallas_call(functools.partial(gather_kernel, chips, group), name='gath...  19.2 us
    pallas_call x1, Pallas kernels, per_device(): pl.pallas_call(functools.partial(reduce_kernel, chips, group), name='redu...  15.5 us
    pallas_call x1, Pallas kernels, per_device(): pl.pallas_call(functools.partial(pair_kernel, group, ring), name='pairs',...  7.65 us

profile of v10, /device:TPU:1, one launch (start us, length us, event | category | flops | bytes accessed | tf_op | source)
XLA Modules:
  0.0 43.6 jit_solution(2812813588498038834)
XLA Ops:
  0.7 19.2 %gather.1 = (f32[8,4,8,128]{3,2,1,0:T(8,128)S(1)}, s32[16,128]{1,0:T(8,128)S(1)}, f32[4,8,4,8,128]{4,3,2,1,0:T(8,128)S(1)}, bf16[8,96,512]{2,1,0:T(8,128)(2,1)S(1)}) custom-call(f32[3,8,128]{2,1,0:T(8,128)} %bitcast.3, f32[8,128]{1,0:T(8,128)} %mass.1, s32[1,1,2,256]{3,2,1,0:T(2,128)} %ids.1, s32[1,1]{1,0:T(1,128)S(6)} %copy.6.count), custom_call_target="tpu_custom_call" | custom-call | tf_op jit(solution)/shard_map/gather/pallas_call | solution.py:377
  19.9 7.7 %pairs.1 = (f32[32,24,128]{2,1,0:T(8,128)S(1)}, f32[2,128,128]{2,1,0:T(8,128)S(1)}) custom-call(s32[16,128]{1,0:T(8,128)S(1)} %get-tuple-element.11.ids, f32[4,8,4,8,128]{4,3,2,1,0:T(8,128)S(1)} %get-tuple-element.12.rows, f32[8,4,8,128]{3,2,1,0:T(8,128)S(1)} %get-tuple-element.13.column, bf16[8,96,512]{2,1,0:T(8,128)(2,1)S(1)} %get-tuple-element.14.choose), custom_call_target="tpu_custom_call" | custom-call | tf_op jit(solution)/shard_map/pairs/pallas_call | solution.py:405
  27.5 15.5 %reduce.1 = f32[3,8,128]{2,1,0:T(8,128)S(1)} custom-call(f32[32,24,128]{2,1,0:T(8,128)S(1)} %get-tuple-element.15.row_force, f32[2,128,128]{2,1,0:T(8,128)S(1)} %get-tuple-element.16.acc), custom_call_target="tpu_custom_call" | custom-call | tf_op jit(solution)/shard_map/reduce/pallas_call | solution.py:422
  43.0 0.6 %copy.7 = f32[8,3,128]{2,0,1:T(8,128)} copy(f32[8,3,128]{2,0,1:T(8,128)S(1)} %bitcast.2) | data formatting | bytes 24576
